TPU v7x, 32 devices: a whole 2x2x4 slice. The times are simulated.
32 devices in a mesh: dp: 16 (over z, x, core), tp: 2 (over y).
Axes of the slice: x: 2, y: 2, z: 4, core: 2. Of those that a mesh axis runs over, the one named last changes fastest.
Arguments:
- tokens: bfloat16 [32768, 768], P(('dp', 'tp')), may hold values from -6 to 6
- masked_positions: int32 [64, 256], P(('dp', 'tp')), may hold values from -1 to 511, as said below
- cotangent: bfloat16 [32768, 768], P(('dp', 'tp')), may hold values from -6 to 6
- query_weight: bfloat16 [768, 768], replicated, may hold values from -0.3125 to 0.3125
- query_bias: float32 [768], replicated, may hold values from -3 to 3
- key_weight: bfloat16 [768, 768], replicated, may hold values from -0.3125 to 0.3125
- value_weight: bfloat16 [768, 768], replicated, may hold values from -0.21875 to 0.21875
- value_bias: float32 [768], replicated, may hold values from -3 to 3
- output_weight: bfloat16 [768, 768], replicated, may hold values from -0.875 to 0.875
- output_bias: float32 [768], replicated, may hold values from -2 to 2
- first_gain: float32 [768], replicated, may hold values from 0.1 to 1.9
- first_shift: float32 [768], replicated, may hold values from -2 to 2
- up_weight: bfloat16 [768, 3072], P(None, 'tp'), may hold values from -0.21875 to 0.21875
- up_bias: float32 [3072], P('tp'), may hold values from -3 to 3
- down_weight: bfloat16 [3072, 768], P('tp'), may hold values from -0.109375 to 0.109375
- lowering_offset: float32 [768], replicated, may hold values from -2 to 2
- second_gain: float32 [768], replicated, may hold values from 0.1 to 1.9
- second_shift: float32 [768], replicated, may hold values from -2 to 2
- channel_filter_scores: bfloat16 [12, 512, 512], P('tp'), may hold values from -6 to 6
- mask_noise: bfloat16 [12, 512, 512], P('tp'), may hold values from -6 to 6
Outputs:
- layer_output: bfloat16 [32768, 768], P(('dp', 'tp'))
- tokens_grad: bfloat16 [32768, 768], P(('dp', 'tp'))
- query_weight_grad: float32 [768, 768], P(None, 'tp')
- query_bias_grad: float32 [768], P('tp')
- key_weight_grad: float32 [768, 768], P(None, 'tp')
- value_weight_grad: float32 [768, 768], P(None, 'tp')
- value_bias_grad: float32 [768], P('tp')
- output_weight_grad: float32 [768, 768], P(None, 'tp')
- output_bias_grad: float32 [768], P('tp')
- first_gain_grad: float32 [768], P('tp')
- first_shift_grad: float32 [768], P('tp')
- up_weight_grad: float32 [768, 3072], P(None, 'tp')
- up_bias_grad: float32 [3072], P('tp')
- down_weight_grad: float32 [3072, 768], P('tp')
- down_bias_grad: float32 [768], P('tp')
- second_gain_grad: float32 [768], P('tp')
- second_shift_grad: float32 [768], P('tp')
- mask_logits_grad: float32 [12, 512, 512], P('tp')
Inputs may be any that keep to these rules, and one draw needn't show every extreme that they name: `masked_positions`: each row lists distinct positions of its sequence in its first slots and -1 in the rest; a row holds 1 to 256 positions, most rows few, and some row exactly 256.
All inputs are finite; a program needn't handle non-finite values.
Results may differ from a plain program's by a relative error of at most 0.017.
The roundings to bfloat16 on the way count: a program that leaves them out, or rounds other values in their place, can miss the bound.
Values may be sent and summed in bfloat16 or wider, within the bound.
No kernel may reach another device: no remote copies, remote signals or barrier semaphores. Data moves between devices by JAX's collectives and lax.ppermute only.
A program may use at most 320 MiB of HBM per device.

v0:
```python
import jax
import jax.numpy as jnp
from jax import lax
from jax.sharding import PartitionSpec as P

relaxation_heat = 0.6
epsilon = 1e-06


def matmul_low(left, right):
    return jnp.dot(left, right, preferred_element_type=jnp.float32)


def norm_forward(hidden, gain, shift):
    centre = hidden - jnp.mean(hidden, -1, keepdims=True)
    spread = jnp.mean(centre * centre, -1, keepdims=True)
    inverse = lax.rsqrt(spread + epsilon)
    normed = centre * inverse
    return (normed * gain + shift, normed, inverse)


def norm_backward(incoming, normed, inverse, gain):
    scaled = incoming * gain
    return inverse * (
        scaled
        - jnp.mean(scaled, -1, keepdims=True)
        - normed * jnp.mean(scaled * normed, -1, keepdims=True)
    )


def local(
    tokens,
    masked_positions,
    cotangent,
    query_weight,
    query_bias,
    key_weight,
    value_weight,
    value_bias,
    output_weight,
    output_bias,
    first_gain,
    first_shift,
    up_weight,
    up_bias,
    down_weight,
    lowering_offset,
    second_gain,
    second_shift,
    channel_filter_scores,
    mask_noise,
):
    row_count, model_width = tokens.shape
    seq_count = masked_positions.shape[0]
    seq_length = row_count // seq_count
    head_count = channel_filter_scores.shape[0] * lax.axis_size("tp")
    head_depth = model_width // head_count
    score_scale = head_depth ** (-0.5)
    query_cols, key_cols, value_cols = (query_weight, key_weight, value_weight)
    query_shift, value_shift = (query_bias, value_bias)
    every_head_logits, every_head_noise = (
        lax.all_gather(channel_filter_scores, "tp", axis=0, tiled=True),
        lax.all_gather(mask_noise, "tp", axis=0, tiled=True),
    )
    switch_levels = jax.nn.sigmoid(
        (every_head_logits.astype(jnp.float32) + every_head_noise.astype(jnp.float32))
        / relaxation_heat
    )
    source_rows = tokens.shape[0]
    shape_heads = (source_rows // seq_length, seq_length, head_count, head_depth)
    queries = (
        (matmul_low(tokens, query_cols) + query_shift).astype(jnp.bfloat16).reshape(shape_heads)
    )
    key_rows = matmul_low(tokens, key_cols).astype(jnp.bfloat16).reshape(shape_heads)
    value_rows = (
        (matmul_low(tokens, value_cols) + value_shift).astype(jnp.bfloat16).reshape(shape_heads)
    )

    def attend(block):
        query_block, key_block, value_block = block
        scores = (
            jnp.einsum("qhd,khd->hqk", query_block, key_block, preferred_element_type=jnp.float32)
            * score_scale
        )
        peak = jnp.max(scores, -1, keepdims=True)
        expo = jnp.exp(scores - peak)
        total = jnp.sum(expo, -1, keepdims=True)
        weights = (expo / total * switch_levels).astype(jnp.bfloat16)
        mixed = jnp.einsum("hqk,khd->qhd", weights, value_block, preferred_element_type=jnp.float32)
        return (mixed.astype(jnp.bfloat16), peak + jnp.log(total))

    context, logsum = lax.map(attend, (queries, key_rows, value_rows))
    context_rows = context.reshape(source_rows, head_count * head_depth)
    attention = matmul_low(context_rows, output_weight) + output_bias
    first_out, first_normed, first_inverse = norm_forward(
        tokens.astype(jnp.float32) + attention, first_gain, first_shift
    )
    gathered = lax.all_gather(first_out.astype(jnp.bfloat16), "tp", axis=0, tiled=True)
    hidden = matmul_low(gathered, up_weight) + up_bias
    active = jax.nn.gelu(hidden, approximate=False).astype(jnp.bfloat16)
    forward = (
        lax.psum_scatter(
            matmul_low(active, down_weight).astype(jnp.bfloat16),
            "tp",
            scatter_dimension=0,
            tiled=True,
        ).astype(jnp.float32)
        + lowering_offset
    )
    final_out, second_normed, second_inverse = norm_forward(
        first_out + forward, second_gain, second_shift
    )
    layer_output = final_out.astype(jnp.bfloat16)
    positions = jnp.arange(seq_length, dtype=jnp.int32)
    chosen = jnp.any(masked_positions[:, :, None] == positions[None, None, :], axis=1).reshape(
        row_count
    )
    grad_out = cotangent.astype(jnp.float32) * chosen[:, None].astype(jnp.float32)
    second_gain_part = jnp.sum(grad_out * second_normed, 0)
    second_shift_part = jnp.sum(grad_out, 0)
    grad_second = norm_backward(grad_out, second_normed, second_inverse, second_gain)
    down_bias_part = jnp.sum(grad_second, 0)
    grad_forward = lax.all_gather(grad_second.astype(jnp.bfloat16), "tp", axis=0, tiled=True)
    grad_active = jnp.einsum(
        "rd,fd->rf", grad_forward, down_weight, preferred_element_type=jnp.float32
    )
    down_weight_part = jnp.einsum(
        "rf,rd->fd", active, grad_forward, preferred_element_type=jnp.float32
    )
    _, gelu_back = jax.vjp(lambda inner: jax.nn.gelu(inner, approximate=False), hidden)
    grad_hidden = gelu_back(grad_active)[0].astype(jnp.bfloat16)
    up_bias_part = jnp.sum(grad_hidden.astype(jnp.float32), 0)
    up_weight_part = jnp.einsum(
        "rd,rf->df", gathered, grad_hidden, preferred_element_type=jnp.float32
    )
    grad_first = grad_second + lax.psum_scatter(
        jnp.einsum("rf,df->rd", grad_hidden, up_weight, preferred_element_type=jnp.float32).astype(
            jnp.bfloat16
        ),
        "tp",
        scatter_dimension=0,
        tiled=True,
    ).astype(jnp.float32)
    first_gain_part = jnp.sum(grad_first * first_normed, 0)
    first_shift_part = jnp.sum(grad_first, 0)
    grad_resid = norm_backward(grad_first, first_normed, first_inverse, first_gain)
    output_bias_part = jnp.sum(grad_resid, 0)
    grad_attention = grad_resid.astype(jnp.bfloat16)
    output_weight_part = jnp.einsum(
        "rc,rd->cd", context_rows, grad_attention, preferred_element_type=jnp.float32
    )
    grad_context = jnp.einsum(
        "rd,cd->rc", grad_attention, output_weight, preferred_element_type=jnp.float32
    ).astype(jnp.bfloat16)
    grad_context = grad_context.reshape(shape_heads)

    def attend_back(switch_total_overall, block):
        query_block, key_block, value_block, logsum_block, grad_block = block
        scores = (
            jnp.einsum("qhd,khd->hqk", query_block, key_block, preferred_element_type=jnp.float32)
            * score_scale
        )
        probs = jnp.exp(scores - logsum_block)
        weights = (probs * switch_levels).astype(jnp.bfloat16)
        grad_values = jnp.einsum(
            "hqk,qhd->khd", weights, grad_block, preferred_element_type=jnp.float32
        )
        grad_weights = jnp.einsum(
            "qhd,khd->hqk", grad_block, value_block, preferred_element_type=jnp.float32
        )
        grad_probs = grad_weights * switch_levels
        grad_scores = (
            probs * (grad_probs - jnp.sum(grad_probs * probs, -1, keepdims=True))
        ).astype(jnp.bfloat16)
        grad_queries = (
            jnp.einsum("hqk,khd->qhd", grad_scores, key_block, preferred_element_type=jnp.float32)
            * score_scale
        )
        grad_keys = (
            jnp.einsum("hqk,qhd->khd", grad_scores, query_block, preferred_element_type=jnp.float32)
            * score_scale
        )
        return (
            switch_total_overall + grad_weights * probs,
            (
                grad_queries.astype(jnp.bfloat16),
                grad_keys.astype(jnp.bfloat16),
                grad_values.astype(jnp.bfloat16),
            ),
        )

    switch_total_overall, (grad_queries, grad_keys, grad_values) = lax.scan(
        attend_back,
        jnp.zeros(switch_levels.shape, jnp.float32),
        (queries, key_rows, value_rows, logsum, grad_context),
    )
    filter_fraction = switch_total_overall * switch_levels * (1.0 - switch_levels) / relaxation_heat
    grad_queries = grad_queries.reshape(source_rows, head_count * head_depth)
    grad_keys = grad_keys.reshape(source_rows, head_count * head_depth)
    grad_values = grad_values.reshape(source_rows, head_count * head_depth)
    query_bias_part = jnp.sum(grad_queries.astype(jnp.float32), 0)
    value_bias_part = jnp.sum(grad_values.astype(jnp.float32), 0)
    query_weight_part = jnp.einsum(
        "rd,re->de", tokens, grad_queries, preferred_element_type=jnp.float32
    )
    key_weight_part = jnp.einsum("rd,re->de", tokens, grad_keys, preferred_element_type=jnp.float32)
    value_weight_part = jnp.einsum(
        "rd,re->de", tokens, grad_values, preferred_element_type=jnp.float32
    )
    input_term = (
        jnp.einsum("re,de->rd", grad_queries, query_cols, preferred_element_type=jnp.float32)
        + jnp.einsum("re,de->rd", grad_keys, key_cols, preferred_element_type=jnp.float32)
        + jnp.einsum("re,de->rd", grad_values, value_cols, preferred_element_type=jnp.float32)
    )
    head_qw, head_qb, head_kw, head_vw, head_vb, head_mask = (
        lax.psum_scatter(
            query_weight_part.astype(jnp.bfloat16), "tp", scatter_dimension=1, tiled=True
        ).astype(jnp.float32),
        lax.psum_scatter(
            query_bias_part.astype(jnp.bfloat16), "tp", scatter_dimension=0, tiled=True
        ).astype(jnp.float32),
        lax.psum_scatter(
            key_weight_part.astype(jnp.bfloat16), "tp", scatter_dimension=1, tiled=True
        ).astype(jnp.float32),
        lax.psum_scatter(
            value_weight_part.astype(jnp.bfloat16), "tp", scatter_dimension=1, tiled=True
        ).astype(jnp.float32),
        lax.psum_scatter(
            value_bias_part.astype(jnp.bfloat16), "tp", scatter_dimension=0, tiled=True
        ).astype(jnp.float32),
        lax.psum_scatter(
            filter_fraction.astype(jnp.bfloat16), "tp", scatter_dimension=0, tiled=True
        ).astype(jnp.float32),
    )
    tokens_grad = (grad_resid + input_term).astype(jnp.bfloat16)
    owner_ow, owner_ob, owner_fg, owner_fs, owner_db, owner_sg, owner_ss = (
        output_weight_part,
        output_bias_part,
        first_gain_part,
        first_shift_part,
        down_bias_part,
        second_gain_part,
        second_shift_part,
    )
    (
        up_weight_grad,
        down_weight_grad,
        up_bias_grad,
        query_weight_grad,
        query_bias_grad,
        key_weight_grad,
        value_weight_grad,
        value_bias_grad,
        mask_logits_grad,
        summed_ow,
        summed_ob,
        summed_fg,
        summed_fs,
        summed_db,
        summed_sg,
        summed_ss,
    ) = lax.psum(
        (
            up_weight_part,
            down_weight_part,
            up_bias_part,
            head_qw,
            head_qb,
            head_kw,
            head_vw,
            head_vb,
            head_mask,
            owner_ow,
            owner_ob,
            owner_fg,
            owner_fs,
            owner_db,
            owner_sg,
            owner_ss,
        ),
        "dp",
    )
    (
        output_weight_grad,
        output_bias_grad,
        first_gain_grad,
        first_shift_grad,
        down_bias_grad,
        second_gain_grad,
        second_shift_grad,
    ) = (
        lax.psum_scatter(
            summed_ow.astype(jnp.bfloat16), "tp", scatter_dimension=1, tiled=True
        ).astype(jnp.float32),
        lax.psum_scatter(
            summed_ob.astype(jnp.bfloat16), "tp", scatter_dimension=0, tiled=True
        ).astype(jnp.float32),
        lax.psum_scatter(
            summed_fg.astype(jnp.bfloat16), "tp", scatter_dimension=0, tiled=True
        ).astype(jnp.float32),
        lax.psum_scatter(
            summed_fs.astype(jnp.bfloat16), "tp", scatter_dimension=0, tiled=True
        ).astype(jnp.float32),
        lax.psum_scatter(
            summed_db.astype(jnp.bfloat16), "tp", scatter_dimension=0, tiled=True
        ).astype(jnp.float32),
        lax.psum_scatter(
            summed_sg.astype(jnp.bfloat16), "tp", scatter_dimension=0, tiled=True
        ).astype(jnp.float32),
        lax.psum_scatter(
            summed_ss.astype(jnp.bfloat16), "tp", scatter_dimension=0, tiled=True
        ).astype(jnp.float32),
    )
    return (
        layer_output,
        tokens_grad,
        query_weight_grad,
        query_bias_grad,
        key_weight_grad,
        value_weight_grad,
        value_bias_grad,
        output_weight_grad,
        output_bias_grad,
        first_gain_grad,
        first_shift_grad,
        up_weight_grad,
        up_bias_grad,
        down_weight_grad,
        down_bias_grad,
        second_gain_grad,
        second_shift_grad,
        mask_logits_grad,
    )


def solution(mesh):
    in_specs = (
        P(("dp", "tp"), None),
        P(("dp", "tp"), None),
        P(("dp", "tp"), None),
        P(),
        P(),
        P(),
        P(),
        P(),
        P(),
        P(),
        P(),
        P(),
        P(None, "tp"),
        P("tp"),
        P("tp", None),
        P(),
        P(),
        P(),
        P("tp", None, None),
        P("tp", None, None),
    )
    out_specs = (
        P(("dp", "tp"), None),
        P(("dp", "tp"), None),
        P(None, "tp"),
        P("tp"),
        P(None, "tp"),
        P(None, "tp"),
        P("tp"),
        P(None, "tp"),
        P("tp"),
        P("tp"),
        P("tp"),
        P(None, "tp"),
        P("tp"),
        P("tp", None),
        P("tp"),
        P("tp"),
        P("tp"),
        P("tp", None, None),
    )
    return jax.shard_map(local, mesh=mesh, in_specs=in_specs, out_specs=out_specs, check_vma=False)
```

profile of v0, /device:TPU:0, one launch (start us, length us, event | category | flops | bytes accessed | tf_op | source)
XLA Modules:
  0.0 1273.2 jit_solution(8404444443663614572)
XLA Ops:
  49.2 43.5 %all-gather.5.cloned.1.call-done = bf16[12,512,512]{2,1,0:T(8,128)(2,1)} async-done(((bf16[6,512,512]{2,1,0:T(8,128)(2,1)}), bf16[12,512,512]{2,1,0:T(8,128)(2,1)}) %all-gather.5.cloned.1.call-update) | async-done | bytes 6291472 | tf_op jit(solution)/shard_map/all_gather | solution.py:62
  92.7 82.0 %all-gather.7.cloned.1.call-done = bf16[12,512,512]{2,1,0:T(8,128)(2,1)} async-done(((bf16[6,512,512]{2,1,0:T(8,128)(2,1)}), bf16[12,512,512]{2,1,0:T(8,128)(2,1)}) %all-gather.7.cloned.1.call-update) | async-done | bytes 6291472 | tf_op jit(solution)/shard_map/all_gather | solution.py:63
  174.6 11.6 add_divide_fusion
  186.2 12.6 copy.143
  200.2 45.6 %while.29 = (s32[]{:T(128)}, bf16[2,512,12,64]{1,3,2,0:T(8,128)(2,1)}, f32[2,12,512,1]{2,1,3,0:T(8,128)}, bf16[2,512,12,64]{1,3,2,0:T(8,128)(2,1)}, bf16[2,512,1...) while((s32[]{:T(128)}, ...), condition=%wide.region_3.4_spmd, body=%wide.region_0.3_spmd.sunk | while | flops 837150720 | bytes 97741496 | solution.py:92
  200.4 7.9 multiply_reduce_fusion.11
  215.7 7.4 fusion.124
  223.1 7.9 multiply_reduce_fusion.11
  238.5 7.4 fusion.124
  254.5 45.0 %all-gather.9.cloned.1.call-done = bf16[2048,768]{0,1:T(8,128)(2,1)} async-done(((bf16[1024,768]{0,1:T(8,128)(2,1)}), bf16[2048,768]{0,1:T(8,128)(2,1)}) %all-gather.9.cloned.1.call-update) | async-done | bytes 3145744 | tf_op jit(solution)/shard_map/all_gather | solution.py:98
  299.6 35.2 %multiply_convert_fusion.20 = (bf16[2048,1536]{1,0:T(8,128)(2,1)S(1)}, f32[2048,1536]{1,0:T(8,128)}, f32[2048,1536]{1,0:T(8,128)}) fusion(f32[1536]{0:T(1024)S(1)} %copy-done.60, bf16[2048,768]{0,1:T(8,128)(2,1)} %all-gather.9.cloned.1.call-done, bf16[768,1536]{1,0:T(8,128)(2,1)S(1)} %copy-done), kind=kOutput, calls=%fused_computation.62 | convolution fusion | flops 5039456256 | bytes 36968448 | tf_op jit(solution)/shard_map/dot_general | solution.py:11
  346.9 40.6 %reduce-scatter.10.cloned.1.call-done = bf16[1024,768]{0,1:T(8,128)(2,1)} async-done(((bf16[2048,768]{0,1:T(8,128)(2,1)}), bf16[1024,768]{0,1:T(8,128)(2,1)}) %reduce-scatter.10.cloned.1.call-update) | async-done | bytes 1572880 | tf_op jit(solution)/shard_map/reduce_scatter | solution.py:102
  397.8 45.0 %all-gather.11.cloned.1.call-done = bf16[2048,768]{0,1:T(8,128)(2,1)} async-done(((bf16[1024,768]{0,1:T(8,128)(2,1)}), bf16[2048,768]{0,1:T(8,128)(2,1)}) %all-gather.11.cloned.1.call-update) | async-done | bytes 3145744 | tf_op jit(solution)/shard_map/all_gather | solution.py:123
  442.8 18.3 %convert_reduce_fusion = (f32[1536]{0:T(1024)}, bf16[2048,1536]{1,0:T(8,128)(2,1)S(1)}) fusion(f32[2048,1536]{1,0:T(8,128)} %get-tuple-element.380, bf16[2048,768]{0,1:T(8,128)(2,1)} %all-gather.11.cloned.1.call-done, bf16[1536,768]{1,0:T(8,128)(2,1)} %param.38, f32[2048,1536]{1,0:T(8,128)} %get-tuple-element.388, f32[1536]{0:T(1024)S(1)} %copy-done.60), kind=kOutput, calls=%fused_computation.60 | convolution fusion | flops 4885314048 | bytes 36974592 | tf_op jit(solution)/shard_map/rd,fd->rf/dot_general | solution.py:124
  470.2 43.4 %reduce-scatter.12.cloned.1.call-done = bf16[1024,768]{0,1:T(8,128)(2,1)} async-done(((bf16[2048,768]{0,1:T(8,128)(2,1)}), bf16[1024,768]{0,1:T(8,128)(2,1)}) %reduce-scatter.12.cloned.1.call-update) | async-done | bytes 1572880 | tf_op jit(solution)/shard_map/reduce_scatter | solution.py:136
  530.4 95.0 %while.30 = (s32[]{:T(128)}, f32[12,512,512]{1,2,0:T(8,128)}, bf16[2,512,12,64]{1,3,2,0:T(8,128)(2,1)}, bf16[2,512,12,64]{1,3,2,0:T(8,128)(2,1)}, bf16[2,512,12,...) while((s32[]{:T(128)}, f32[12,512,512]{1,2,0:T(8,128)}, ...), condition=%wide.region_17.18_spmd.clone, body=%wide.region_15.17_spmd.clone.sunk | while | flops 2068703232 | bytes 196793648 | solution.py:192
  530.6 7.8 fusion.132
  538.4 18.1 %multiply_reduce_fusion.12 = (f32[12,512]{1,0:T(8,128)S(1)}, f32[12,512,512]{1,2,0:T(8,128)}, f32[12,512,512]{1,2,0:T(8,128)}, f32[12,512,512]{1,2,0:T(8,128)S(1)}) fusion(f32[12,512]{1,0:T(8,128)S(1)} %dynamic-slice_bitcast_fusion.2, f32[12,512,512]{1,2,0:T(8,128)} %fusion.132, f32[12,512,512]{1,2,0:T(8,128)} %get-tuple-element.575, ...), kind=kOutput, calls=%fused_computation.22.clone.1 | convolution fusion | flops 427812864 | bytes 77128704 | tf_op jit(solution)/shard_map/while/body/eval_jaxpr/qhd,khd->hqk/dot_general | solution.py:160
  556.5 7.0 multiply_convert_fusion.26
  567.9 8.4 fusion.135
  576.3 7.8 fusion.132
  584.1 21.5 %multiply_reduce_fusion.12 = (f32[12,512]{1,0:T(8,128)S(1)}, f32[12,512,512]{1,2,0:T(8,128)}, f32[12,512,512]{1,2,0:T(8,128)}, f32[12,512,512]{1,2,0:T(8,128)S(1)}) fusion(f32[12,512]{1,0:T(8,128)S(1)} %dynamic-slice_bitcast_fusion.2, f32[12,512,512]{1,2,0:T(8,128)} %fusion.132, f32[12,512,512]{1,2,0:T(8,128)} %get-tuple-element.575, ...), kind=kOutput, calls=%fused_computation.22.clone.1 | convolution fusion | flops 427812864 | bytes 77128704 | tf_op jit(solution)/shard_map/while/body/eval_jaxpr/qhd,khd->hqk/dot_general | solution.py:160
  617.0 8.4 fusion.135
  638.5 12.8 %copy.160 = f32[12,512,512]{2,1,0:T(8,128)} copy(f32[12,512,512]{1,2,0:T(8,128)} %get-tuple-element.121) | data formatting | bytes 25165824 | tf_op jit(solution)/shard_map/while | solution.py:192
  657.0 13.3 %multiply_convert_fusion.19 = bf16[12,512,512]{2,1,0:T(8,128)(2,1)} fusion(f32[12,512,512]{2,1,0:T(8,128)} %copy.160, bf16[12,512,512]{2,1,0:T(8,128)(2,1)} %all-gather.7.cloned.1.call-done, bf16[12,512,512]{2,1,0:T(8,128)(2,1)} %all-gather.5.cloned.1.call-done), kind=kLoop, calls=%fused_computation.59 | loop fusion | flops 37748736 | bytes 31457280 | tf_op jit(solution)/shard_map/convert_element_type | solution.py:232
  683.1 20.7 %reduce-scatter.18.cloned.1.call-done = bf16[768,384]{0,1:T(8,128)(2,1)} async-done(((bf16[768,768]{0,1:T(8,128)(2,1)}), bf16[768,384]{0,1:T(8,128)(2,1)}) %reduce-scatter.18.cloned.1.call-update) | async-done | bytes 589840 | tf_op jit(solution)/shard_map/reduce_scatter | solution.py:225
  703.8 79.9 %reduce-scatter.20.cloned.1.call-done = bf16[6,512,512]{2,1,0:T(8,128)(2,1)} async-done(((bf16[12,512,512]{2,1,0:T(8,128)(2,1)}), bf16[6,512,512]{2,1,0:T(8,128)(2,1)}) %reduce-scatter.20.cloned.1.call-update) | async-done | bytes 3145744 | tf_op jit(solution)/shard_map/reduce_scatter | solution.py:231
  783.7 257.9 %all-reduce.16 = (f32[768,384]{0,1:T(8,128)}, f32[384]{0:T(512)}, f32[768,384]{0,1:T(8,128)}, f32[768,384]{0,1:T(8,128)}, f32[384]{0:T(512)}, /*index=5*/bf16[76...) all-reduce(bf16[768,384]{0,1:T(8,128)(2,1)} %reduce-scatter.14.clon, ...), channel_id=1, replica_groups=mesh['dp'=16,'tp'=2] {'dp'}, use_global_device_ids=true, to_apply=%region_19.20 | all-reduce | flops 3054336 | bytes 18330624 | tf_op jit(solution)/shard_map/psum | solution.py:262
  1043.2 9.7 fusion.69
  1052.9 9.4 fusion.68
  1079.5 7.6 all-reduce.10
  1093.5 165.0 %all-reduce.15.cloned.1.call-done = (f32[768,1536]{1,0:T(8,128)}, f32[1536,768]{1,0:T(8,128)}) async-done(((f32[768,1536]{1,0:T(8,128)}, f32[1536,768]{1,0:T(8,128)}), (f32[768,1536]{1,0:T(8,128)}, f32[1536,768]{1,0:T(8,128)})) %all-reduce.15.cloned.1.call-update) | async-done | bytes 9437200 | tf_op jit(solution)/shard_map/psum | solution.py:262
  (287 shorter events, 193.6 us)
Async XLA Ops:
  7.2 292.4 %copy-start = (bf16[768,1536]{1,0:T(8,128)(2,1)S(1)}, bf16[768,1536]{1,0:T(8,128)(2,1)}, u32[]{:S(2)}) copy-start(bf16[768,1536]{1,0:T(8,128)(2,1)} %param.36) | copy-start | bytes 7077892
  7.2 85.5 %all-gather.5.cloned.1.call-start = ((), (), s32[]{:S(2)}) async-start(), calls=%async_computation.7 | async-start | bytes 9437184 | tf_op jit(solution)/shard_map/all_gather | solution.py:62
  8.0 166.7 %all-gather.7.cloned.1.call-start = ((), (), s32[]{:S(2)}) async-start(), calls=%async_computation.8 | async-start | bytes 9437184 | tf_op jit(solution)/shard_map/all_gather | solution.py:63
  8.7 290.9 %all-gather.9.cloned.1.call-start = ((), (), s32[]{:S(2)}) async-start(), calls=%async_computation.9 | async-start | bytes 4718592 | tf_op jit(solution)/shard_map/all_gather | solution.py:98
  200.3 15.4 %slice-start = ((s8[12582912]{0:T(1024)(128)(4,1)}), s8[4194304]{0:T(1024)(128)(4,1)S(1)}, s32[]{:S(2)}) async-start(s8[12582912]{0:T(1024)(128)(4,1)} %bitcast.175), calls=%async_computation.19 | async-start | bytes 8388608 | tf_op jit(solution)/shard_map/while
  200.3 15.4 %slice-start.1 = ((s8[12582912]{0:T(1024)(128)(4,1)}), s8[4194304]{0:T(1024)(128)(4,1)S(1)}, s32[]{:S(2)}) async-start(s8[12582912]{0:T(1024)(128)(4,1)} %bitcast.175), calls=%async_computation.20 | async-start | bytes 8388608 | tf_op jit(solution)/shard_map/while
  208.2 7.5 slice-start.2
  208.2 7.5 copy-start.7
  223.1 15.4 %slice-start = ((s8[12582912]{0:T(1024)(128)(4,1)}), s8[4194304]{0:T(1024)(128)(4,1)S(1)}, s32[]{:S(2)}) async-start(s8[12582912]{0:T(1024)(128)(4,1)} %bitcast.175), calls=%async_computation.19 | async-start | bytes 8388608 | tf_op jit(solution)/shard_map/while
  223.1 15.4 %slice-start.1 = ((s8[12582912]{0:T(1024)(128)(4,1)}), s8[4194304]{0:T(1024)(128)(4,1)S(1)}, s32[]{:S(2)}) async-start(s8[12582912]{0:T(1024)(128)(4,1)} %bitcast.175), calls=%async_computation.20 | async-start | bytes 8388608 | tf_op jit(solution)/shard_map/while
  231.0 7.5 slice-start.2
  231.0 7.5 copy-start.7
  252.8 46.8 %copy-start.60 = (f32[1536]{0:T(1024)S(1)}, f32[1536]{0:T(1024)}, u32[]{:S(2)}) copy-start(f32[1536]{0:T(1024)} %param.37) | copy-start | bytes 18436
  254.5 133.1 %reduce-scatter.10.cloned.1.call-start = ((), (), s32[]{:S(2)}) async-start(), calls=%async_computation.10 | async-start | bytes 4718592 | tf_op jit(solution)/shard_map/reduce_scatter | solution.py:102
  299.6 37.8 %copy-start.54 = (bf16[1536,768]{1,0:T(8,128)(2,1)S(1)}, bf16[1536,768]{1,0:T(8,128)(2,1)}, u32[]{:S(2)}) copy-start(bf16[1536,768]{1,0:T(8,128)(2,1)} %param.38) | copy-start | bytes 7077892
  344.0 43.5 %copy-start.44 = (f32[768]{0:T(1024)S(1)}, f32[768]{0:T(1024)}, u32[]{:S(2)}) copy-start(f32[768]{0:T(1024)} %param.39) | copy-start | bytes 9220
  344.0 98.8 %all-gather.11.cloned.1.call-start = ((), (), s32[]{:S(2)}) async-start(), calls=%async_computation.11 | async-start | bytes 4718592 | tf_op jit(solution)/shard_map/all_gather | solution.py:123
  397.8 115.9 %reduce-scatter.12.cloned.1.call-start = ((), (), s32[]{:S(2)}) async-start(), calls=%async_computation.12 | async-start | bytes 4718592 | tf_op jit(solution)/shard_map/reduce_scatter | solution.py:136
  470.1 43.5 %copy-start.5 = (f32[1024,768]{0,1:T(8,128)S(1)}, f32[1024,768]{0,1:T(8,128)}, u32[]{:S(2)}) copy-start(f32[1024,768]{0,1:T(8,128)} %copy-done.4) | copy-start | bytes 9437188
  470.2 212.9 %reduce-scatter.14.cloned.1.call-start = ((), (), s32[]{:S(2)}) async-start(), calls=%async_computation.13 | async-start | bytes 1769472 | tf_op jit(solution)/shard_map/reduce_scatter | solution.py:216
  632.6 50.5 %reduce-scatter.16.cloned.1.call-start = ((), (), s32[]{:S(2)}) async-start(), calls=%async_computation.14 | async-start | bytes 1769472 | tf_op jit(solution)/shard_map/reduce_scatter | solution.py:222
  638.4 65.3 %reduce-scatter.18.cloned.1.call-start = ((), (), s32[]{:S(2)}) async-start(), calls=%async_computation.15 | async-start | bytes 1769472 | tf_op jit(solution)/shard_map/reduce_scatter | solution.py:225
  638.5 12.8 %copy-start.11 = (bf16[2,512,12,64]{1,3,2,0:T(8,128)(2,1)S(1)}, bf16[2,512,12,64]{1,3,2,0:T(8,128)(2,1)}, u32[]{:S(2)}) copy-start(bf16[2,512,12,64]{1,3,2,0:T(8,128)(2,1)} %get-tuple-element.120) | copy-start | bytes 4718596
  657.0 126.7 %reduce-scatter.20.cloned.1.call-start = ((), (), s32[]{:S(2)}) async-start(), calls=%async_computation.16 | async-start | bytes 9437184 | tf_op jit(solution)/shard_map/reduce_scatter | solution.py:231
  670.4 420.6 %reduce-scatter.22.cloned.1.call-start = ((), (), s32[]{:S(2)}) async-start(), calls=%async_computation.17 | async-start | bytes 1769472
  673.0 110.7 %copy-start.40 = (f32[768]{0:T(1024)S(1)}, f32[768]{0:T(1024)}, u32[]{:S(2)}) copy-start(f32[768]{0:T(1024)} %get-tuple-element.304) | copy-start | bytes 9220
  673.0 110.7 %copy-start.41 = (f32[768]{0:T(1024)S(1)}, f32[768]{0:T(1024)}, u32[]{:S(2)}) copy-start(f32[768]{0:T(1024)} %get-tuple-element.310) | copy-start | bytes 9220
  673.0 110.7 %copy-start.42 = (f32[768]{0:T(1024)S(1)}, f32[768]{0:T(1024)}, u32[]{:S(2)}) copy-start(f32[768]{0:T(1024)} %get-tuple-element.302) | copy-start | bytes 9220
  673.0 110.7 %copy-start.43 = (f32[768]{0:T(1024)S(1)}, f32[768]{0:T(1024)}, u32[]{:S(2)}) copy-start(f32[768]{0:T(1024)} %get-tuple-element.307) | copy-start | bytes 9220
  1043.1 9.8 copy-start.53
  1043.1 215.4 %all-reduce.15.cloned.1.call-start = ((), (), s32[]{:S(2)}) async-start(), calls=%async_computation.18 | async-start | bytes 18874368 | tf_op jit(solution)/shard_map/psum | solution.py:262
  1258.5 7.4 copy-start.1
  (61 other events, 200.5 us)
Sparse Core Ops, SparseCore 0:
  9.6 83.0 all-gather.4
  94.2 80.3 all-gather.6
  254.6 44.9 all-gather.8
  344.2 43.3 reduce-scatter.9
  397.9 44.9 all-gather.10
  470.3 43.3 reduce-scatter.11
  632.7 21.7 reduce-scatter.13
  657.4 21.7 reduce-scatter.15
  682.0 21.7 reduce-scatter.17
  706.6 77.0 reduce-scatter.19
  1043.2 25.4 reduce-scatter.21
  1073.3 185.1 all-reduce.14
where the time goes:
time: 1280 us; the launch traced here: 1270 us
  waiting for transfers between devices  567 us (44%)
  blocking collectives  270 us (21%)
  matrix products  223 us (17%)
  local copies, waits for them, and re-layouts  117 us (9%)
  other arithmetic  78.2 us (6%)
  between operations  15.9 us (1%)
    psum x1, blocking collectives, local(): lax.psum((up_weight_part, down_weight_part, up_bias_part, head_qw, head_q...  258 us
    psum x1, waiting for transfers between devices, local(): lax.psum((up_weight_part, down_weight_part, up_bias_part, head_qw, head_q...  165 us
    all_gather x1, waiting for transfers between devices, local(): lax.all_gather(mask_noise, 'tp', axis=0, tiled=True)  82 us
    reduce_scatter x1, waiting for transfers between devices, local(): lax.psum_scatter(filter_fraction.astype(jnp.bfloat16), 'tp', scatter_dime...  79.9 us
    dot_general x6, matrix products, matmul_low(): return jnp.dot(left, right, preferred_element_type=jnp.float32)  52.5 us
    all_gather x1, waiting for transfers between devices, local(): lax.all_gather(grad_second.astype(jnp.bfloat16), 'tp', axis=0, tiled=True)  45 us
    all_gather x1, waiting for transfers between devices, local(): lax.all_gather(first_out.astype(jnp.bfloat16), 'tp', axis=0, tiled=True)  45 us
    unnamed x144, local copies, waits for them, and re-layouts  43.9 us
  transfers between devices with their start and end apart: 12, of which 9 were waited for; matrix products, arithmetic and copies ran while one was open for 10% of the time, Pallas kernels for 0%

commit v1 on v0

v1 whole, which is shorter than its diff:
```python
import functools

import jax
import jax.numpy as jnp
from jax import lax
from jax.experimental import pallas as pl
from jax.experimental.pallas import tpu as pltpu
from jax.sharding import PartitionSpec as P

heat = 0.6
epsilon = 1e-06
low = jnp.bfloat16
full = jnp.float32
MIB = 1 << 20


def dot(left, right, left_dim=1, right_dim=0):
    return lax.dot_general(
        left, right, (((left_dim,), (right_dim,)), ((), ())), preferred_element_type=full
    )


def shape(dims, kind):
    return jax.ShapeDtypeStruct(dims, kind)


def params(mib=40):
    return pltpu.CompilerParams(vmem_limit_bytes=mib * MIB)


def cost(flops, moved, special=0):
    return pl.CostEstimate(flops=int(flops), bytes_accessed=int(moved), transcendentals=int(special))


def head_lanes(width):
    lane = lax.broadcasted_iota(jnp.int32, (1, width), 1)
    first = lane < width // 2
    return first, (first.astype(full).astype(low), (1.0 - first.astype(full)).astype(low))


def attend_kernel(place, q_ref, k_ref, v_ref, *rest):
    gates, (context_ref, logsum_ref) = rest[:4], rest[-2:]
    rows = gates[0].shape[1]
    first, lanes = head_lanes(q_ref.shape[1])
    keys, values = k_ref[...], v_ref[...]
    for r, gate_ref in enumerate(gates):
        start = pl.multiple_of((place[1] ^ r) * rows, rows)
        tile = pl.ds(start, rows)
        queries = q_ref[tile, :]
        mixed, logs = [], []
        for h in range(2):
            scores = dot(queries * lanes[h], keys, 1, 1)
            peak = jnp.max(scores, -1, keepdims=True)
            expo = jnp.exp(scores - peak)
            total = jnp.sum(expo, -1, keepdims=True)
            weights = (expo * gate_ref[h].astype(full)).astype(low)
            mixed.append(dot(weights, values) * (1.0 / total))
            logs.append(peak + jnp.log(total))
        context_ref[tile, :] = jnp.where(first, mixed[0], mixed[1]).astype(low)
        logsum_ref[tile, :] = jnp.where(first, logs[0], logs[1])


def attend(place, queries, keys, values, gates, own, earlier, length):
    rows, width = queries.shape
    pairs, part = gates[0].shape[0] // 2, length // 4
    lanes = 128
    seqs = rows // length
    column = pl.BlockSpec((length, lanes), lambda hp, s, place: (s, place[0] + hp))
    if own:
        gate_specs = [
            pl.BlockSpec((2, part, length), lambda hp, s, place, r=r: (hp, place[1] ^ r, 0))
            for r in range(4)
        ]
    else:
        gate_specs = [
            pl.BlockSpec((2, part, length), lambda hp, s, place: (hp, 0, 0)) for r in range(4)
        ]
    return pl.pallas_call(
        attend_kernel,
        grid_spec=pltpu.PrefetchScalarGridSpec(
            num_scalar_prefetch=1,
            grid=(pairs, seqs),
            in_specs=[column] * 3
            + gate_specs
            + [pl.BlockSpec(memory_space=pl.ANY)] * len(earlier),
            out_specs=[column, column],
        ),
        out_shape=[shape((rows, width), low), shape((rows, width), full)],
        input_output_aliases={8 + i: i for i in range(len(earlier))},
        compiler_params=params(),
        cost_estimate=cost(
            8 * seqs * pairs * length * length * lanes,
            rows * width * 5,
            2 * seqs * pairs * length * length,
        ),
        name="attend",
    )(place, queries, keys, values, *gates, *earlier)


def attend_back_kernel(place, scale, q_ref, k_ref, v_ref, d_ref, logsum_ref, *rest):
    gates = rest[:4]
    grads_ref, mask_ref, sums_ref, mask_acc, weights_all, slopes_all = rest[4:]
    s, hp = pl.program_id(0), pl.program_id(1)
    rows = gates[0].shape[1]
    width = q_ref.shape[1]
    group = grads_ref.shape[1] // 3
    first, lanes = head_lanes(width)
    keys, values = k_ref[...], v_ref[...]
    grad_q = grad_k = grad_v = None
    for h in range(2):
        for r, gate_ref in enumerate(gates):
            start = pl.multiple_of((place[1] ^ r) * rows, rows)
            tile = pl.ds(start, rows)
            scores = dot(q_ref[tile, :] * lanes[h], keys, 1, 1)
            probs = jnp.exp(scores - logsum_ref[tile, h * (width // 2) : h * (width // 2) + 1])
            grad_weights = dot(d_ref[tile, :] * lanes[h], values, 1, 1)
            gate = gate_ref[h].astype(full)
            part = grad_weights * probs
            place_of = (hp * 2 + h, tile)

            @pl.when(s == 0)
            def _():
                mask_acc[place_of] = part

            @pl.when(s > 0)
            def _():
                mask_acc[place_of] += part

            gated = part * gate
            slopes = gated - probs * jnp.sum(gated, -1, keepdims=True)
            weights_all[tile, :] = (probs * gate).astype(low)
            slopes_all[tile, :] = slopes.astype(low)
        weights, slopes = weights_all[...], slopes_all[...]
        new_v = dot(weights, d_ref[...] * lanes[h], 0, 0)
        new_q = dot(slopes, keys * lanes[h])
        new_k = dot(slopes, q_ref[...] * lanes[h], 0, 0)
        if h == 0:
            grad_q, grad_k, grad_v = new_q, new_k, new_v
        else:
            grad_q, grad_k, grad_v = grad_q + new_q, grad_k + new_k, grad_v + new_v
    grad_q = (grad_q * scale).astype(low)
    grad_k, grad_v = grad_k.astype(low), grad_v.astype(low)
    for n, grad in enumerate((grad_q, grad_k, grad_v)):
        at = pl.multiple_of(n * group + hp * width, width)
        grads_ref[:, pl.ds(at, width)] = grad
    at = pl.ds(pl.multiple_of(hp * width, width), width)
    column = jnp.concatenate(
        [
            jnp.sum(grad_q.astype(full), 0, keepdims=True),
            jnp.sum(grad_v.astype(full), 0, keepdims=True),
            jnp.zeros((6, width), full),
        ],
        0,
    )

    @pl.when(s == 0)
    def _():
        sums_ref[:, at] = column

    @pl.when(s > 0)
    def _():
        sums_ref[:, at] += column

    @pl.when(s == pl.num_programs(0) - 1)
    def _():
        for h in range(2):
            mask_ref[h] = mask_acc[hp * 2 + h].astype(low)


def attend_back(place, queries, keys, values, grad_context, logsum, gates, own, length, scale):
    rows, width = queries.shape
    heads, part = gates[0].shape[0], length // 4
    pairs, lanes, seqs = heads // 2, 128, rows // length
    column = pl.BlockSpec((length, lanes), lambda s, hp, place: (s, place[0] + hp))
    if own:
        gate_specs = [
            pl.BlockSpec((2, part, length), lambda s, hp, place, r=r: (hp, place[1] ^ r, 0))
            for r in range(4)
        ]
    else:
        gate_specs = [
            pl.BlockSpec((2, part, length), lambda s, hp, place: (hp, 0, 0)) for r in range(4)
        ]
    group = pairs * lanes

    def kernel(place, *refs):
        attend_back_kernel(place, scale, *refs)

    return pl.pallas_call(
        kernel,
        grid_spec=pltpu.PrefetchScalarGridSpec(
            num_scalar_prefetch=1,
            grid=(seqs, pairs),
            in_specs=[column] * 5 + gate_specs,
            out_specs=[
                pl.BlockSpec((length, 3 * group), lambda s, hp, place: (s, 0)),
                pl.BlockSpec(
                    (2, length, length),
                    lambda s, hp, place: (jnp.where(s == seqs - 1, hp, 0), 0, 0),
                ),
                pl.BlockSpec((8, group), lambda s, hp, place: (0, 0)),
            ],
            scratch_shapes=[
                pltpu.VMEM((heads, length, length), full),
                pltpu.VMEM((length, length), low),
                pltpu.VMEM((length, length), low),
            ],
        ),
        out_shape=[
            shape((rows, 3 * group), low),
            shape((heads, length, length), low),
            shape((8, group), full),
        ],
        compiler_params=params(),
        cost_estimate=cost(
            20 * seqs * pairs * length * length * lanes,
            rows * width * 12,
            2 * seqs * pairs * length * length,
        ),
        name="attend_back",
    )(place, queries, keys, values, grad_context, logsum, *gates)


def norm_forward(hidden, gain, shift):
    centre = hidden - jnp.mean(hidden, -1, keepdims=True)
    spread = jnp.mean(centre * centre, -1, keepdims=True)
    inverse = lax.rsqrt(spread + epsilon)
    normed = centre * inverse
    return normed * gain + shift, normed, inverse


def norm_backward(incoming, normed, inverse, gain):
    scaled = incoming * gain
    return inverse * (
        scaled
        - jnp.mean(scaled, -1, keepdims=True)
        - normed * jnp.mean(scaled * normed, -1, keepdims=True)
    )


def add_rows(ref, rows):
    packed = jnp.concatenate(
        [jnp.sum(row, 0, keepdims=True) for row in rows]
        + [jnp.zeros((8 - len(rows), ref.shape[1]), full)],
        0,
    )

    @pl.when(pl.program_id(0) == 0)
    def _():
        ref[...] = packed

    @pl.when(pl.program_id(0) > 0)
    def _():
        ref[...] += packed


def first_norm_kernel(
    slots_ref, context_ref, tokens_ref, weight_ref, bias_ref, gain_ref, shift_ref,
    order_ref, picked_ref, compact_ref, low_ref, normed_ref, inverse_ref,
):
    length, slots = tokens_ref.shape[0], slots_ref.shape[-1]
    position = lax.broadcasted_iota(jnp.int32, (length, slots), 0)
    hit = (position == slots_ref[0]).astype(full)
    chosen = jnp.max(hit, -1, keepdims=True)
    row = lax.broadcasted_iota(jnp.int32, (length, length), 0)
    column = lax.broadcasted_iota(jnp.int32, (length, length), 1)
    lower = (column <= row).astype(full).astype(low)
    upto = dot(lower, jnp.broadcast_to(chosen, (length, 128)).astype(low))[:, :1]
    count = jnp.sum(chosen, 0, keepdims=True)
    at = lax.broadcasted_iota(jnp.int32, (length, 1), 0).astype(full)
    target = jnp.where(chosen > 0, upto - 1.0, count + at - upto)
    order = (column.astype(full) == target).astype(full)
    picked_ref[...] = (order * chosen)[:, :slots].astype(low)
    order = order.astype(low)
    order_ref[...] = order
    context = dot(order, context_ref[...], 0, 0).astype(low)
    tokens = dot(order, tokens_ref[...], 0, 0)
    compact_ref[...] = context[:slots]
    attention = dot(context, weight_ref[...]) + bias_ref[...]
    out, normed, inverse = norm_forward(tokens + attention, gain_ref[...], shift_ref[...])
    low_ref[...] = out.astype(low)
    normed_ref[...] = normed
    inverse_ref[...] = jnp.broadcast_to(inverse[:slots], (slots, 128))


def first_norm(positions, context, tokens, weight, bias, gain, shift, length):
    rows, width = tokens.shape
    seqs, slots = positions.shape
    by_seq = lambda n, w: pl.BlockSpec((n, w), lambda s: (s, 0))
    whole = lambda a: pl.BlockSpec(a.shape, lambda s: (0,) * a.ndim)
    return pl.pallas_call(
        first_norm_kernel,
        grid=(seqs,),
        in_specs=[
            pl.BlockSpec((1, 1, slots), lambda s: (s, 0, 0)),
            by_seq(length, width),
            by_seq(length, width),
            whole(weight),
            whole(bias),
            whole(gain),
            whole(shift),
        ],
        out_specs=[
            by_seq(length, length),
            by_seq(length, slots),
            by_seq(slots, width),
            by_seq(length, width),
            by_seq(length, width),
            by_seq(slots, 128),
        ],
        out_shape=[
            shape((rows, length), low),
            shape((rows, slots), low),
            shape((seqs * slots, width), low),
            shape((rows, width), low),
            shape((rows, width), full),
            shape((seqs * slots, 128), full),
        ],
        compiler_params=params(),
        cost_estimate=cost(2 * rows * width * (width + 2 * length), rows * width * 12),
        name="first_norm",
    )(positions[:, None, :], context, tokens, weight, bias, gain, shift)


def gelu_parts(hidden):
    size = jnp.abs(hidden)
    t = 1.0 / (1.0 + (0.3275911 * 0.7071067811865476) * size)
    poly = 1.061405429 * t - 1.453152027
    poly = poly * t + 1.421413741
    poly = poly * t - 0.284496736
    poly = poly * t + 0.254829592
    bell = jnp.exp(hidden * hidden * -0.5)
    tail = 0.5 * poly * t * bell
    below = jnp.where(hidden > 0, 1.0 - tail, tail)
    return below, bell


def forward_kernel(place, x_ref, *refs, chained, per_seq):
    weights, refs = refs[:6], refs[6:]
    if chained:
        start_ref, refs = refs[0], refs[1:]
    total_ref, active_refs, slope_refs = refs[0], refs[1:3], refs[3:5]
    x = x_ref[...]
    step = 256

    def body(keep):
        total = start_ref[...] if chained else None
        for r in range(2):
            up, down, bias = weights[3 * r : 3 * r + 3]
            for c in range(0, up.shape[1], step):
                hidden = dot(x, up[:, c : c + step]) + bias[:, c : c + step]
                below, bell = gelu_parts(hidden)
                active = (hidden * below).astype(low)
                if keep:
                    active_refs[r][:, c : c + step] = active
                    slope_refs[r][:, c : c + step] = below + hidden * bell * 0.3989422804014327
                term = dot(active, down[c : c + step, :])
                total = term if total is None else total + term
        total_ref[...] = total

    i = pl.program_id(0)

    @pl.when(lax.rem(i, per_seq) == 0)
    def _():
        body(True)

    @pl.when(lax.rem(i, per_seq) != 0)
    def _():
        body(False)


def weight_specs(width, half, sliced):
    specs = []
    for r in range(2):
        if sliced:
            specs += [
                pl.BlockSpec((width, half), lambda i, place, r=r: (0, place[2] ^ r)),
                pl.BlockSpec((half, width), lambda i, place, r=r: (place[2] ^ r, 0)),
                pl.BlockSpec((1, half), lambda i, place, r=r: (0, place[2] ^ r)),
            ]
        else:
            specs += [
                pl.BlockSpec((width, half), lambda i, place: (0, 0)),
                pl.BlockSpec((half, width), lambda i, place: (0, 0)),
                pl.BlockSpec((1, half), lambda i, place: (0, 0)),
            ]
    return specs


def forward(place, x, pieces, sliced, start, length, slots):
    rows, width = x.shape
    half = pieces[0].shape[1] // (2 if sliced else 1)
    per_seq = length // slots
    kept = rows // per_seq
    block = pl.BlockSpec((slots, width), lambda i, place: (i, 0))
    kept_block = pl.BlockSpec((slots, half), lambda i, place: (i // per_seq, 0))
    extra = [] if start is None else [start]
    return pl.pallas_call(
        functools.partial(forward_kernel, chained=bool(extra), per_seq=per_seq),
        grid_spec=pltpu.PrefetchScalarGridSpec(
            num_scalar_prefetch=1,
            grid=(rows // slots,),
            in_specs=[block] + weight_specs(width, half, sliced) + [block] * len(extra),
            out_specs=[block] + [kept_block] * 4,
        ),
        out_shape=[shape((rows, width), full)]
        + [shape((kept, half), low)] * 2
        + [shape((kept, half), full)] * 2,
        compiler_params=params(),
        cost_estimate=cost(
            8 * rows * width * half, rows * width * 16 + half * width * 8, 4 * rows * half
        ),
        name="forward",
    )(place, x, *pieces, *extra)


def second_norm_kernel(
    total_ref, normed_ref, cotangent_ref, order_ref, picked_ref,
    offset_ref, gain1_ref, shift1_ref, gain2_ref, shift2_ref,
    out_ref, grad_ref, low_ref, sums_ref,
):
    slots = picked_ref.shape[1]
    first_out = normed_ref[...] * gain1_ref[...] + shift1_ref[...]
    gain = gain2_ref[...]
    out, normed, inverse = norm_forward(
        first_out + (total_ref[...] + offset_ref[...]), gain, shift2_ref[...]
    )
    out_ref[...] = dot(order_ref[...], out.astype(low)).astype(low)
    grad_out = dot(picked_ref[...], cotangent_ref[...], 0, 0)
    normed, inverse = normed[:slots], inverse[:slots]
    grad = norm_backward(grad_out, normed, inverse, gain)
    grad_ref[...] = grad
    low_ref[...] = grad.astype(low)
    add_rows(sums_ref, (grad_out * normed, grad_out, grad))


def second_norm(total, normed, cotangent, order, picked, offset, gain1, shift1, gain2, shift2):
    rows, width = total.shape
    length, slots = order.shape[1], picked.shape[1]
    seqs = rows // length
    by_seq = lambda n, w: pl.BlockSpec((n, w), lambda s: (s, 0))
    vector = pl.BlockSpec((1, width), lambda s: (0, 0))
    return pl.pallas_call(
        second_norm_kernel,
        grid=(seqs,),
        in_specs=[
            by_seq(length, width),
            by_seq(length, width),
            by_seq(length, width),
            by_seq(length, length),
            by_seq(length, slots),
        ]
        + [vector] * 5,
        out_specs=[
            by_seq(length, width),
            by_seq(slots, width),
            by_seq(slots, width),
            pl.BlockSpec((8, width), lambda s: (0, 0)),
        ],
        out_shape=[
            shape((rows, width), low),
            shape((seqs * slots, width), full),
            shape((seqs * slots, width), low),
            shape((8, width), full),
        ],
        compiler_params=params(),
        cost_estimate=cost(2 * rows * width * (length + slots), rows * width * 16),
        name="second_norm",
    )(total, normed, cotangent, order, picked, offset, gain1, shift1, gain2, shift2)


def backward_kernel(place, grad_ref, *refs, chained):
    weights, refs = refs[:6], refs[6:]
    slope_refs, refs = refs[:2], refs[2:]
    if chained:
        start_ref, refs = refs[0], refs[1:]
    total_ref, hidden_refs, sums_ref = refs[0], refs[1:3], refs[3]
    grad = grad_ref[...]
    total = start_ref[...] if chained else None
    step = 256
    half = weights[0].shape[1]
    i = pl.program_id(0)

    @pl.when(i == 0)
    def _():
        sums_ref[...] = jnp.zeros_like(sums_ref)

    for r in range(2):
        up, down, _ = weights[3 * r : 3 * r + 3]
        for c in range(0, half, step):
            grad_active = dot(grad, down[c : c + step, :], 1, 1)
            grad_hidden = (grad_active * slope_refs[r][:, c : c + step]).astype(low)
            hidden_refs[r][:, c : c + step] = grad_hidden
            sums_ref[r : r + 1, c : c + step] += jnp.sum(grad_hidden.astype(full), 0, keepdims=True)
            term = dot(grad_hidden, up[:, c : c + step], 1, 1)
            total = term if total is None else total + term
    total_ref[...] = total


def backward(place, grad, pieces, sliced, slopes, start, block_rows):
    rows, width = grad.shape
    half = slopes[0].shape[1]
    block = pl.BlockSpec((block_rows, width), lambda i, place: (i, 0))
    wide = pl.BlockSpec((block_rows, half), lambda i, place: (i, 0))
    extra = [] if start is None else [start]
    return pl.pallas_call(
        functools.partial(backward_kernel, chained=bool(extra)),
        grid_spec=pltpu.PrefetchScalarGridSpec(
            num_scalar_prefetch=1,
            grid=(rows // block_rows,),
            in_specs=[block]
            + weight_specs(width, half, sliced)
            + [wide] * 2
            + [block] * len(extra),
            out_specs=[block, wide, wide, pl.BlockSpec((8, half), lambda i, place: (0, 0))],
        ),
        out_shape=[shape((rows, width), full)]
        + [shape((rows, half), low)] * 2
        + [shape((8, half), full)],
        compiler_params=params(),
        cost_estimate=cost(8 * rows * width * half, rows * width * 20 + half * width * 8),
        name="backward",
    )(place, grad, *pieces, *slopes, *extra)


def first_back_kernel(
    total_ref, second_ref, normed_ref, inverse_ref, gain_ref, weight_ref, picked_ref,
    resid_ref, low_ref, context_ref, sums_ref,
):
    grad_first = second_ref[...] + total_ref[...]
    normed = normed_ref[...]
    resid = norm_backward(grad_first, normed, inverse_ref[:, :1], gain_ref[...])
    upper = resid.astype(low)
    lower = (resid - upper.astype(full)).astype(low)
    low_ref[...] = upper
    picked = picked_ref[...]
    resid_ref[...] = dot(picked, upper) + dot(picked, lower)
    grad_context = dot(upper, weight_ref[...], 1, 1).astype(low)
    context_ref[...] = dot(picked, grad_context).astype(low)
    add_rows(sums_ref, (grad_first * normed, grad_first, resid))


def first_back(total, second, normed, inverse, gain, weight, picked, length):
    rows, width = normed.shape
    slots = picked.shape[1]
    seqs, per_seq = rows // length, length // slots
    by_seq = lambda n, w: pl.BlockSpec((n, w), lambda s: (s, 0))
    whole = lambda a: pl.BlockSpec(a.shape, lambda s: (0,) * a.ndim)
    return pl.pallas_call(
        first_back_kernel,
        grid=(seqs,),
        in_specs=[
            by_seq(slots, width),
            by_seq(slots, width),
            pl.BlockSpec((slots, width), lambda s: (s * per_seq, 0)),
            by_seq(slots, 128),
            whole(gain),
            whole(weight),
            by_seq(length, slots),
        ],
        out_specs=[
            by_seq(length, width),
            by_seq(slots, width),
            by_seq(length, width),
            pl.BlockSpec((8, width), lambda s: (0, 0)),
        ],
        out_shape=[
            shape((rows, width), full),
            shape((seqs * slots, width), low),
            shape((rows, width), low),
            shape((8, width), full),
        ],
        compiler_params=params(),
        cost_estimate=cost(2 * rows * width * (width + slots), rows * width * 12),
        name="first_back",
    )(total, second, normed, inverse, gain, weight, picked)


def input_kernel(place, resid_ref, own_ref, other_ref, *refs):
    weights, out_ref = refs[:6], refs[6]
    total = resid_ref[...]
    group = weights[0].shape[1]
    for side, grads in enumerate((own_ref, other_ref)):
        for n in range(3):
            total += dot(grads[:, n * group : (n + 1) * group], weights[3 * side + n][...], 1, 1)
    out_ref[...] = total.astype(low)


def input_grad(place, resid, own, other, weights):
    rows, width = resid.shape
    group = own.shape[1] // 3
    block_rows = 256
    block = pl.BlockSpec((block_rows, width), lambda i, place: (i, 0))
    wide = pl.BlockSpec((block_rows, 3 * group), lambda i, place: (i, 0))
    specs = [
        pl.BlockSpec((width, group), lambda i, place, side=side: (0, place[3] ^ side))
        for side in range(2)
        for n in range(3)
    ]
    return pl.pallas_call(
        input_kernel,
        grid_spec=pltpu.PrefetchScalarGridSpec(
            num_scalar_prefetch=1,
            grid=(rows // block_rows,),
            in_specs=[block, wide, wide] + specs,
            out_specs=block,
        ),
        out_shape=shape((rows, width), low),
        compiler_params=params(),
        cost_estimate=cost(12 * rows * width * group, rows * width * 12),
        name="input_grad",
    )(place, resid, own, other, *weights, *weights)


def make_local(n_dp):
    bits = n_dp.bit_length() - 1

    def swap(a, bit):
        return lax.ppermute(a, "dp", [(i, i ^ (1 << bit)) for i in range(n_dp)])

    def swap_tp(a):
        return lax.ppermute(a, "tp", [(0, 1), (1, 0)])

    def added(a, b):
        return (a.astype(full) + b.astype(full)).astype(low)

    def in_order(mine, other, bit, axis):
        return jnp.concatenate(
            [jnp.where(bit == 0, mine, other), jnp.where(bit == 0, other, mine)], axis
        )

    def local(
        tokens,
        masked_positions,
        cotangent,
        query_weight,
        query_bias,
        key_weight,
        value_weight,
        value_bias,
        output_weight,
        output_bias,
        first_gain,
        first_shift,
        up_weight,
        up_bias,
        down_weight,
        lowering_offset,
        second_gain,
        second_shift,
        channel_filter_scores,
        mask_noise,
    ):
        rows, width = tokens.shape
        seqs, slots = masked_positions.shape
        length = rows // seqs
        own_heads = channel_filter_scores.shape[0]
        depth = width // (2 * own_heads)
        scale = depth ** (-0.5)
        pairs = own_heads * depth // 128
        half = up_weight.shape[1] // 2
        dp, tp = lax.axis_index("dp"), lax.axis_index("tp")
        bit = [(dp >> b) & 1 for b in range(bits)]
        quarter = 2 * bit[0] + bit[1]

        def place(side):
            return jnp.stack([(tp ^ side) * pairs, quarter, bit[0], tp]).astype(jnp.int32)

        own, other = place(0), place(1)

        def halves(a, axis, which):
            n = a.shape[axis] // 2
            return lax.dynamic_slice_in_dim(a, which * n, n, axis)

        def quarter_of(a, axis):
            n = a.shape[axis] // 4
            return lax.dynamic_slice_in_dim(a, quarter * n, n, axis)

        gate = jax.nn.sigmoid(
            (channel_filter_scores.astype(full) + mask_noise.astype(full)) / heat
        ).astype(low)
        gate_0 = swap_tp(quarter_of(gate, 1))
        gate_1 = swap(gate_0, 1)
        gate_2, gate_3 = swap(gate_0, 0), swap(gate_1, 0)
        other_gates = (gate_0, gate_1, gate_2, gate_3)
        own_gates = (gate,) * 4

        up_q, down_q = swap_tp(quarter_of(up_weight, 1)), swap_tp(quarter_of(down_weight, 0))
        bias_o = swap_tp(up_bias)
        up_near = in_order(up_q, swap(up_q, 1), bit[1], 1)
        down_near = in_order(down_q, swap(down_q, 1), bit[1], 0)
        up_far, down_far = swap(up_near, 0), swap(down_near, 0)
        bias_own = up_bias[None, :]
        bias_near = halves(bias_o, 0, bit[0])[None, :]
        bias_far = halves(bias_o, 0, 1 - bit[0])[None, :]
        own_pieces = (up_weight, down_weight, bias_own) * 2
        other_pieces = (up_near, down_near, bias_near, up_far, down_far, bias_far)

        row = lambda v: v[None, :]

        queries = ((dot(tokens, query_weight) + query_bias).astype(low).astype(full) * scale).astype(
            low
        )
        keys = dot(tokens, key_weight).astype(low)
        values = (dot(tokens, value_weight) + value_bias).astype(low)
        earlier = attend(own, queries, keys, values, own_gates, True, [], length)
        context, logsum = attend(
            other, queries, keys, values, other_gates, False, earlier, length
        )

        order, picked, context_c, x, normed, inverse = first_norm(
            masked_positions,
            context,
            tokens,
            output_weight,
            row(output_bias),
            row(first_gain),
            row(first_shift),
            length,
        )
        total, own_a0, own_a1, own_s0, own_s1 = forward(
            own, x, own_pieces, True, None, length, slots
        )
        total, far_a0, far_a1, far_s0, far_s1 = forward(
            other, x, other_pieces, False, total, length, slots
        )
        layer_output, grad_second, grad_forward, sums_second = second_norm(
            total,
            normed,
            cotangent,
            order,
            picked,
            row(lowering_offset),
            row(first_gain),
            row(first_shift),
            row(second_gain),
            row(second_shift),
        )

        def reduce_rows(mine, axis):
            for b in range(1, bits):
                keep, send = halves(mine, axis, bit[b]), halves(mine, axis, 1 - bit[b])
                mine = added(keep, swap(send, b))
            for b in range(bits - 1, 0, -1):
                mine = in_order(mine, swap(mine, b), bit[b], axis)
            return mine

        def reduce_chunk(grad, axis, final_axis):
            send_far, send_own = grad(1, 1).astype(low), grad(0, 1).astype(low)
            got_far, got_own = swap(send_far, 0), swap(send_own, 0)
            keep_far = (grad(1, 0) + got_far.astype(full)).astype(low)
            got = swap_tp(keep_far)
            keep_own = (grad(0, 0) + got_own.astype(full) + got.astype(full)).astype(low)
            mine = reduce_rows(keep_own, axis)
            return in_order(mine, swap(mine, 0), bit[0], final_axis)

        actives = ((own_a0, own_a1), (far_a0, far_a1))
        down_grad = reduce_chunk(
            lambda side, r: dot(actives[side][r], grad_forward, 0, 0), 0, 0
        )

        back, own_h0, own_h1, own_sums = backward(
            own, grad_forward, own_pieces, True, (own_s0, own_s1), None, slots
        )
        back, far_h0, far_h1, far_sums = backward(
            other, grad_forward, other_pieces, False, (far_s0, far_s1), back, slots
        )
        x_c = x.reshape(seqs, length, width)[:, :slots].reshape(seqs * slots, width)
        hiddens = ((own_h0, own_h1), (far_h0, far_h1))
        up_grad = reduce_chunk(lambda side, r: dot(x_c, hiddens[side][r], 0, 0), 0, 1)

        resid, grad_attention, grad_context, sums_first = first_back(
            back, grad_second, normed, inverse, row(first_gain), output_weight, picked, length
        )
        context_h = [halves(context_c, 1, bit[0]), halves(context_c, 1, 1 - bit[0])]
        attention_h = [halves(grad_attention, 1, tp), halves(grad_attention, 1, 1 - tp)]
        output_grad = reduce_chunk(
            lambda side, r: dot(context_h[r], attention_h[side], 0, 0), 0, 0
        )

        grads_far, mask_far, sums_far = attend_back(
            other, queries, keys, values, grad_context, logsum, other_gates, False, length, scale
        )
        grads_own, mask_own, sums_own = attend_back(
            own, queries, keys, values, grad_context, logsum, own_gates, True, length, scale
        )
        masks = (mask_own, mask_far)
        mask_grad = reduce_chunk(
            lambda side, r: halves(masks[side], 1, bit[0] ^ r).astype(full), 1, 1
        )
        tokens_h = [halves(tokens, 1, bit[0]), halves(tokens, 1, 1 - bit[0])]
        grads_all = (grads_own, grads_far)
        qkv_grad = reduce_chunk(lambda side, r: dot(tokens_h[r], grads_all[side], 0, 0), 0, 0)
        tokens_grad = input_grad(
            own, resid, grads_own, grads_far, (query_weight, key_weight, value_weight)
        )

        def both(mine, theirs):
            return in_order(mine, theirs, tp, 0)

        def hidden_half(sums):
            return in_order(sums[0], sums[1], bit[0], 0)

        vectors = jnp.concatenate(
            [
                both(hidden_half(own_sums), hidden_half(far_sums)),
                both(sums_own[0], sums_far[0]),
                both(sums_own[1], sums_far[1]),
                sums_first[0],
                sums_first[1],
                sums_first[2],
                sums_second[0],
                sums_second[1],
                sums_second[2],
            ]
        ).reshape(-1, 128)
        vectors = vectors + swap_tp(vectors)
        for b in range(bits):
            vectors = vectors + swap(vectors, b)
        vectors = vectors.reshape(-1)
        hidden_all = 4 * half
        up_bias_grad = halves(vectors[:hidden_all], 0, tp)
        rest = vectors[hidden_all:].reshape(-1, width)
        rest = halves(rest, 1, tp)
        query_bias_grad, value_bias_grad, fg, fs, ob, sg, ss, db = [rest[i] for i in range(8)]

        group = own_heads * depth
        qkv_grad = qkv_grad.astype(full)
        exact = jax.nn.sigmoid(
            (channel_filter_scores.astype(full) + mask_noise.astype(full)) / heat
        )
        return (
            layer_output,
            tokens_grad,
            qkv_grad[:, :group],
            query_bias_grad,
            qkv_grad[:, group : 2 * group],
            qkv_grad[:, 2 * group :],
            value_bias_grad,
            output_grad.astype(full),
            ob,
            fg,
            fs,
            up_grad.astype(full),
            up_bias_grad,
            down_grad.astype(full),
            db,
            sg,
            ss,
            mask_grad.astype(full) * exact * (1.0 - exact) / heat,
        )

    return local


def solution(mesh):
    in_specs = (
        P(("dp", "tp"), None),
        P(("dp", "tp"), None),
        P(("dp", "tp"), None),
        P(),
        P(),
        P(),
        P(),
        P(),
        P(),
        P(),
        P(),
        P(),
        P(None, "tp"),
        P("tp"),
        P("tp", None),
        P(),
        P(),
        P(),
        P("tp", None, None),
        P("tp", None, None),
    )
    out_specs = (
        P(("dp", "tp"), None),
        P(("dp", "tp"), None),
        P(None, "tp"),
        P("tp"),
        P(None, "tp"),
        P(None, "tp"),
        P("tp"),
        P(None, "tp"),
        P("tp"),
        P("tp"),
        P("tp"),
        P(None, "tp"),
        P("tp"),
        P("tp", None),
        P("tp"),
        P("tp"),
        P("tp"),
        P("tp", None, None),
    )
    local = make_local(mesh.shape["dp"])
    return jax.shard_map(local, mesh=mesh, in_specs=in_specs, out_specs=out_specs, check_vma=False)
```

time: 1280 us -> 561 us (0.44)
  waiting for transfers between devices: 567 us -> 236 us
  blocking collectives: 270 us -> 0 us
  matrix products: 223 us -> 34.3 us
  Pallas kernels: 0 us -> 140 us
  local copies, waits for them, and re-layouts: 117 us -> 59.8 us
  other arithmetic: 78.2 us -> 29.3 us
  starting transfers between devices: 0.7 us -> 49.2 us
  between operations: 15.9 us -> 2.42 us
    psum x1 -> x0, blocking collectives: 258 us -> none  [local(): lax.psum((up_weight_part, down_weight_part, up_bias_part, head_qw, head_q...]
    ppermute x0 -> x66, waiting for transfers between devices: none -> 236 us  [the longest x56 147 us: swap(): return lax.ppermute(a, 'dp', [(i, i ^ 1 << bit) for i in range(n_dp)])]
    all_gather x4 -> x0, waiting for transfers between devices: 216 us -> none  [the longest x1 82 us: local(): lax.all_gather(mask_noise, 'tp', axis=0, tiled=True)]
    dot_general x32 -> x19, matrix products: 223 us -> 34.3 us  [dot(): lax.dot_general(left, right, (((left_dim,), (right_dim,)), ((), ())), pre...]
    reduce_scatter x6 -> x0, waiting for transfers between devices: 185 us -> none  [the longest x1 79.9 us: local(): lax.psum_scatter(filter_fraction.astype(jnp.bfloat16), 'tp', scatter_dime...]
    psum x1 -> x0, waiting for transfers between devices: 165 us -> none  [local(): lax.psum((up_weight_part, down_weight_part, up_bias_part, head_qw, head_q...]
    pallas_call x0 -> x12, Pallas kernels: none -> 140 us  [the longest x2 49 us: attend_back(): pl.pallas_call(kernel, grid_spec=pltpu.PrefetchScalarGridSpec(num_scalar_...]
    ppermute x0 -> x66, starting transfers between devices: none -> 49.2 us  [the longest x56 38.7 us: swap(): return lax.ppermute(a, 'dp', [(i, i ^ 1 << bit) for i in range(n_dp)])]
  transfers between devices with their start and end apart: 12 -> 66, of which waited for: 9 -> 29; matrix products, arithmetic and copies ran while one was open for 10% -> 12% of each run, Pallas kernels for 0% -> 11%
where the time goes in v1:
time: 561 us; the launch traced here: 551 us
  waiting for transfers between devices  236 us (42%)
  Pallas kernels  140 us (25%)
  local copies, waits for them, and re-layouts  59.8 us (11%)
  starting transfers between devices  49.2 us (9%)
  matrix products  34.3 us (6%)
  other arithmetic  29.3 us (5%)
    ppermute x56, waiting for transfers between devices, swap(): return lax.ppermute(a, 'dp', [(i, i ^ 1 << bit) for i in range(n_dp)])  147 us
    ppermute x10, waiting for transfers between devices, swap_tp(): return lax.ppermute(a, 'tp', [(0, 1), (1, 0)])  89.1 us
    pallas_call x2, Pallas kernels, attend_back(): pl.pallas_call(kernel, grid_spec=pltpu.PrefetchScalarGridSpec(num_scalar_...  49 us
    unnamed x195, local copies, waits for them, and re-layouts  46.5 us
    ppermute x56, starting transfers between devices, swap(): return lax.ppermute(a, 'dp', [(i, i ^ 1 << bit) for i in range(n_dp)])  38.7 us
    dot_general x19, matrix products, dot(): lax.dot_general(left, right, (((left_dim,), (right_dim,)), ((), ())), pre...  34.3 us
    pallas_call x2, Pallas kernels, attend(): pl.pallas_call(attend_kernel, grid_spec=pltpu.PrefetchScalarGridSpec(num_...  32.9 us
    pallas_call x2, Pallas kernels, forward(): pl.pallas_call(functools.partial(forward_kernel, chained=bool(extra), per...  25.5 us
  transfers between devices with their start and end apart: 66, of which 29 were waited for; matrix products, arithmetic and copies ran while one was open for 12% of the time, Pallas kernels for 11%

profile of v1, /device:TPU:0, one launch (start us, length us, event | category | flops | bytes accessed | tf_op | source)
XLA Modules:
  0.0 551.4 jit_solution(13052037710452157959)
XLA Ops:
  24.6 24.2 %collective-permute-done.4 = bf16[768,384]{1,0:T(8,128)(2,1)} collective-permute-done((bf16[768,384]{1,0:T(8,128)(2,1)S(1)}, bf16[768,384]{1,0:T(8,128)(2,1)}, u32[]{:S(2)}, u32[]{:S(2)}) %collective-permute-start.4) | collective-permute-done | bytes 589856 | tf_op jit(solution)/shard_map/ppermute | solution.py:622
  56.4 24.0 %collective-permute-done.1.rest_1_.refs_6_ = bf16[6,128,512]{2,1,0:T(8,128)(2,1)} collective-permute-done((bf16[6,128,512]{2,1,0:T(8,128)(2,1)}, bf16[6,128,512]{2,1,0:T(8,128)(2,1)}, u32[]{:S(2)}, u32[]{:S(2)}) %collective-permute-start.1) | collective-permute-done | bytes 786464 | tf_op jit(solution)/shard_map/ppermute | solution.py:619
  87.7 16.0 %attend.2 = (bf16[1024,768]{1,0:T(8,128)(2,1)S(1)}, f32[1024,768]{1,0:T(8,128)S(1)}) custom-call(s32[4]{0:T(128)S(1)} %add_add_fusion.1.place, bf16[1024,768]{1,0:T(8,128)(2,1)S(1)} %copy-done.5, bf16[1024,768]{1,0:T(8,128)(2,1)S(1)} %copy-done.8, bf16[1024,768]{1,0:T(8,128)(2,1)S(1)} %copy-done.2, ...), custom_call_target="tpu_custom_call" | custom-call | flops 1610612736 | bytes 3932160 | tf_op jit(solution)/shard_map/attend/pallas_call | solution.py:78
  114.4 16.9 %attend.3 = (bf16[1024,768]{1,0:T(8,128)(2,1)S(1)}, f32[1024,768]{1,0:T(8,128)S(1)}) custom-call(s32[4]{0:T(128)S(1)} %add_add_fusion.place, bf16[1024,768]{1,0:T(8,128)(2,1)S(1)} %copy-done.6, bf16[1024,768]{1,0:T(8,128)(2,1)S(1)} %copy-done.9, bf16[1024,768]{1,0:T(8,128)(2,1)S(1)} %copy-done.3, ...), custom_call_target="tpu_custom_call", output_to_operand_aliasing={{0}: (8, {}), {1}: (9, {})} | custom-call | flops 1610612736 | bytes 3932160 | tf_op jit(solution)/shard_map/attend/pallas_call | solution.py:78
  135.5 5.8 %first_norm.1 = (bf16[1024,512]{1,0:T(8,128)(2,1)S(1)}, bf16[1024,256]{1,0:T(8,128)(2,1)S(1)}, bf16[512,768]{1,0:T(8,128)(2,1)S(1)}, bf16[1024,768]{1,0:T(8,128)...) custom-call(s32[2,1,256]{2,1,0:T(1,128)S(1)} %broadcast_in_dim.35.slots_ref, ...), custom_call_target="tpu_custom_call" | custom-call | flops 2818572288 | bytes 9437184 | tf_op jit(solution)/shard_map/first_norm/pallas_call | solution.py:291
  141.3 13.4 %forward.2 = (f32[1024,768]{1,0:T(8,128)S(1)}, bf16[512,768]{1,0:T(8,128)(2,1)S(1)}, bf16[512,768]{1,0:T(8,128)(2,1)S(1)}, f32[512,768]{1,0:T(8,128)S(1)}, f32[512,768]{1,0:T(8,128)S(1)}) custom-call(s32[4]{0:T(128)S(1)} %add_add_fusion.1.place, bf16[1024,768]{1,0:T(8,128)(2,1)S(1)} %get-tuple-element.63.x_ref, bf16[768,1536]{1,0:T(8,128)(2,1)S(1)} %copy-done.14, ...), custom_call_target="tpu_custom_call" | custom-call | flops 4831838208 | bytes 17301504 | tf_op jit(solution)/shard_map/forward/pallas_call | solution.py:398
  160.4 12.1 %forward.3 = (f32[1024,768]{1,0:T(8,128)S(1)}, bf16[512,768]{1,0:T(8,128)(2,1)S(1)}, bf16[512,768]{1,0:T(8,128)(2,1)S(1)}, f32[512,768]{1,0:T(8,128)S(1)}, f32[512,768]{1,0:T(8,128)S(1)}) custom-call(s32[4]{0:T(128)S(1)} %add_add_fusion.place, bf16[1024,768]{1,0:T(8,128)(2,1)S(1)} %get-tuple-element.63.x_ref, bf16[768,768]{1,0:T(8,128)(2,1)} %pad_maximum_fusion.1.refs_0_, ...), custom_call_target="tpu_custom_call" | custom-call | flops 4831838208 | bytes 17301504 | tf_op jit(solution)/shard_map/forward/pallas_call | solution.py:398
  184.1 5.1 backward.2
  194.1 6.6 %backward.3 = (f32[512,768]{1,0:T(8,128)S(1)}, bf16[512,768]{1,0:T(8,128)(2,1)S(1)}, bf16[512,768]{1,0:T(8,128)(2,1)S(1)}, f32[8,768]{1,0:T(8,128)S(1)}) custom-call(s32[4]{0:T(128)S(1)} %add_add_fusion.place, bf16[512,768]{1,0:T(8,128)(2,1)S(1)} %get-tuple-element.70.grad_ref, bf16[768,768]{1,0:T(8,128)(2,1)} %pad_maximum_fusion.1.refs_0_, ...), custom_call_target="tpu_custom_call" | custom-call | flops 2415919104 | bytes 12582912 | tf_op jit(solution)/shard_map/backward/pallas_call | solution.py:506
  209.5 24.0 %attend_back.2 = (bf16[1024,1152]{1,0:T(8,128)(2,1)S(1)}, bf16[6,512,512]{2,1,0:T(8,128)(2,1)S(1)}, f32[8,384]{1,0:T(8,128)S(1)}) custom-call(s32[4]{0:T(128)S(1)} %add_add_fusion.1.place, bf16[1024,768]{1,0:T(8,128)(2,1)S(1)} %copy-done.7, bf16[1024,768]{1,0:T(8,128)(2,1)S(1)} %copy-done.10, bf16[1024,768]{1,0:T(8,128)(2,1)S(1)} %copy-done.4, ...), custom_call_target="tpu_custom_call" | custom-call | flops 4026531840 | bytes 9437184 | tf_op jit(solution)/shard_map/attend_back/pallas_call | solution.py:189
  233.4 25.1 %attend_back.3 = (bf16[1024,1152]{1,0:T(8,128)(2,1)S(1)}, bf16[6,512,512]{2,1,0:T(8,128)(2,1)}, f32[8,384]{1,0:T(8,128)S(1)}) custom-call(s32[4]{0:T(128)S(1)} %add_add_fusion.place, bf16[1024,768]{1,0:T(8,128)(2,1)S(1)} %copy-done.7, bf16[1024,768]{1,0:T(8,128)(2,1)S(1)} %copy-done.10, bf16[1024,768]{1,0:T(8,128)(2,1)S(1)} %copy-done.4, ...), custom_call_target="tpu_custom_call" | custom-call | flops 4026531840 | bytes 9437184 | tf_op jit(solution)/shard_map/attend_back/pallas_call | solution.py:189
  273.8 7.8 %input_grad.1 = bf16[1024,768]{1,0:T(8,128)(2,1)} custom-call(s32[4]{0:T(128)S(1)} %add_add_fusion.1.place, f32[1024,768]{1,0:T(8,128)S(1)} %copy-done.27, bf16[1024,1152]{1,0:T(8,128)(2,1)S(1)} %get-tuple-element.82.own_ref, bf16[1024,1152]{1,0:T(8,128)(2,1)S(1)} %get-tuple-element.83.other_ref, bf16[768,768]{1,0:T(8,128)(2,1)S(1)} %copy-done.21, ...), custom_call_target="tpu_custom_call" | custom-call | flops 3623878656 | bytes 9437184 | tf_op jit(solution)/shard_map/input_grad/pallas_call | solution.py:600
  288.7 6.4 %collective-permute-done.28 = bf16[384,384]{1,0:T(8,128)(2,1)S(1)} collective-permute-done((bf16[384,384]{1,0:T(8,128)(2,1)S(1)}, bf16[384,384]{1,0:T(8,128)(2,1)S(1)}, u32[]{:S(2)}, u32[]{:S(2)}) %collective-permute-start.28) | collective-permute-done | bytes 294944 | tf_op jit(solution)/shard_map/ppermute | solution.py:622
  330.0 12.4 %collective-permute-done.13 = bf16[384,1152]{1,0:T(8,128)(2,1)S(1)} collective-permute-done((bf16[384,1152]{1,0:T(8,128)(2,1)S(1)}, bf16[384,1152]{1,0:T(8,128)(2,1)S(1)}, u32[]{:S(2)}, u32[]{:S(2)}) %collective-permute-start.13) | collective-permute-done | bytes 884768 | tf_op jit(solution)/shard_map/ppermute | solution.py:622
  349.1 8.4 %collective-permute-done.14 = bf16[192,1152]{1,0:T(8,128)(2,1)S(1)} collective-permute-done((bf16[192,1152]{1,0:T(8,128)(2,1)S(1)}, bf16[192,1152]{1,0:T(8,128)(2,1)S(1)}, u32[]{:S(2)}, u32[]{:S(2)}) %collective-permute-start.14) | collective-permute-done | bytes 442400 | tf_op jit(solution)/shard_map/ppermute | solution.py:619
  367.1 19.2 %collective-permute-done.48 = bf16[768,768]{1,0:T(8,128)(2,1)S(1)} collective-permute-done((bf16[768,768]{1,0:T(8,128)(2,1)S(1)}, bf16[768,768]{1,0:T(8,128)(2,1)S(1)}, u32[]{:S(2)}, u32[]{:S(2)}) %collective-permute-start.48) | collective-permute-done | bytes 1179680 | tf_op jit(solution)/shard_map/ppermute | solution.py:622
  387.9 7.2 %collective-permute-done.16 = bf16[48,1152]{1,0:T(8,128)(2,1)S(1)} collective-permute-done((bf16[48,1152]{1,0:T(8,128)(2,1)S(1)}, bf16[48,1152]{1,0:T(8,128)(2,1)S(1)}, u32[]{:S(2)}, u32[]{:S(2)}) %collective-permute-start.16) | collective-permute-done | bytes 110624 | tf_op jit(solution)/shard_map/ppermute | solution.py:619
  395.2 5.7 %collective-permute-done.17 = bf16[48,1152]{1,0:T(8,128)(2,1)S(1)} collective-permute-done((bf16[48,1152]{1,0:T(8,128)(2,1)S(1)}, bf16[48,1152]{1,0:T(8,128)(2,1)S(1)}, u32[]{:S(2)}, u32[]{:S(2)}) %collective-permute-start.17) | collective-permute-done | bytes 110624 | tf_op jit(solution)/shard_map/ppermute | solution.py:619
  402.7 9.0 %collective-permute-done.38 = bf16[768,768]{1,0:T(8,128)(2,1)S(1)} collective-permute-done((bf16[768,768]{1,0:T(8,128)(2,1)S(1)}, bf16[768,768]{1,0:T(8,128)(2,1)S(1)}, u32[]{:S(2)}, u32[]{:S(2)}) %collective-permute-start.38) | collective-permute-done | bytes 1179680 | tf_op jit(solution)/shard_map/ppermute | solution.py:622
  415.5 12.9 %collective-permute-done.39 = bf16[384,768]{1,0:T(8,128)(2,1)S(1)} collective-permute-done((bf16[384,768]{1,0:T(8,128)(2,1)S(1)}, bf16[384,768]{1,0:T(8,128)(2,1)S(1)}, u32[]{:S(2)}, u32[]{:S(2)}) %collective-permute-start.39) | collective-permute-done | bytes 589856 | tf_op jit(solution)/shard_map/ppermute | solution.py:619
  429.6 14.5 %collective-permute-done.58 = bf16[6,256,512]{2,1,0:T(8,128)(2,1)S(1)} collective-permute-done((bf16[6,256,512]{2,1,0:T(8,128)(2,1)S(1)}, bf16[6,256,512]{2,1,0:T(8,128)(2,1)S(1)}, u32[]{:S(2)}, u32[]{:S(2)}) %collective-permute-start.58) | collective-permute-done | bytes 1572896 | tf_op jit(solution)/shard_map/ppermute | solution.py:622
  450.0 8.6 %collective-permute-done.51 = bf16[96,768]{1,0:T(8,128)(2,1)S(1)} collective-permute-done((bf16[96,768]{1,0:T(8,128)(2,1)S(1)}, bf16[96,768]{1,0:T(8,128)(2,1)S(1)}, u32[]{:S(2)}, u32[]{:S(2)}) %collective-permute-start.51) | collective-permute-done | bytes 147488 | tf_op jit(solution)/shard_map/ppermute | solution.py:619
  458.7 7.8 %collective-permute-done.41 = bf16[96,768]{1,0:T(8,128)(2,1)S(1)} collective-permute-done((bf16[96,768]{1,0:T(8,128)(2,1)S(1)}, bf16[96,768]{1,0:T(8,128)(2,1)S(1)}, u32[]{:S(2)}, u32[]{:S(2)}) %collective-permute-start.41) | collective-permute-done | bytes 147488 | tf_op jit(solution)/shard_map/ppermute | solution.py:619
  466.6 4.6 collective-permute-done.52
  476.5 4.8 collective-permute-done.53
  482.1 7.7 %collective-permute-done.60 = bf16[6,64,512]{2,1,0:T(8,128)(2,1)S(1)} collective-permute-done((bf16[6,64,512]{2,1,0:T(8,128)(2,1)S(1)}, bf16[6,64,512]{2,1,0:T(8,128)(2,1)S(1)}, u32[]{:S(2)}, u32[]{:S(2)}) %collective-permute-start.60) | collective-permute-done | bytes 393248 | tf_op jit(solution)/shard_map/ppermute | solution.py:619
  490.0 6.9 %collective-permute-done.43 = bf16[192,768]{1,0:T(8,128)(2,1)S(1)} collective-permute-done((bf16[192,768]{1,0:T(8,128)(2,1)S(1)}, bf16[192,768]{1,0:T(8,128)(2,1)S(1)}, u32[]{:S(2)}, u32[]{:S(2)}) %collective-permute-start.43) | collective-permute-done | bytes 294944 | tf_op jit(solution)/shard_map/ppermute | solution.py:619
  497.7 4.1 collective-permute-done.61
  502.3 6.2 %collective-permute-done.62 = bf16[6,32,512]{2,1,0:T(8,128)(2,1)S(1)} collective-permute-done((bf16[6,32,512]{2,1,0:T(8,128)(2,1)S(1)}, bf16[6,32,512]{2,1,0:T(8,128)(2,1)S(1)}, u32[]{:S(2)}, u32[]{:S(2)}) %collective-permute-start.62) | collective-permute-done | bytes 196640 | tf_op jit(solution)/shard_map/ppermute | solution.py:619
  509.1 8.0 %collective-permute-done.63 = bf16[6,64,512]{2,1,0:T(8,128)(2,1)S(1)} collective-permute-done((bf16[6,64,512]{2,1,0:T(8,128)(2,1)S(1)}, bf16[6,64,512]{2,1,0:T(8,128)(2,1)S(1)}, u32[]{:S(2)}, u32[]{:S(2)}) %collective-permute-start.63) | collective-permute-done | bytes 393248 | tf_op jit(solution)/shard_map/ppermute | solution.py:619
  520.0 15.2 %collective-permute-done.64 = bf16[6,128,512]{2,1,0:T(8,128)(2,1)S(1)} collective-permute-done((bf16[6,128,512]{2,1,0:T(8,128)(2,1)S(1)}, bf16[6,128,512]{2,1,0:T(8,128)(2,1)S(1)}, u32[]{:S(2)}, u32[]{:S(2)}) %collective-permute-start.64) | collective-permute-done | bytes 786464 | tf_op jit(solution)/shard_map/ppermute | solution.py:619
  546.9 4.3 multiply_multiply_fusion
  (443 shorter events, 194.3 us)
Async XLA Ops:
  9.4 41.1 %collective-permute-start = (bf16[6,128,512]{2,1,0:T(8,128)(2,1)S(1)}, bf16[6,128,512]{2,1,0:T(8,128)(2,1)}, u32[]{:S(2)}, u32[]{:S(2)}) collective-permute-start(bf16[6,128,512]{2,1,0:T(8,128)(2,1)S(1)} %constant_dynamic-slice_fusion.20), channel_id=1, source_target_pairs={{0,1},{1,0},{2,3},{3,2},{4,5},{5,4},{6,7},{7,6},{8,9},{9,8},{10,11... | collective-permute-start | bytes 2359304 | tf_op jit(solution)/shard_map/ppermute | solution.py:622
  11.9 36.9 %collective-permute-start.4 = (bf16[768,384]{1,0:T(8,128)(2,1)S(1)}, bf16[768,384]{1,0:T(8,128)(2,1)}, u32[]{:S(2)}, u32[]{:S(2)}) collective-permute-start(bf16[768,384]{1,0:T(8,128)(2,1)S(1)} %constant_dynamic-slice_fusion.19), channel_id=1, source_target_pairs={{0,1},{1,0},{2,3},{3,2},{4,5},{5,4},{6,7},{7,6},{8,9},{9,8},{10,11... | collective-permute-start | bytes 1769480 | tf_op jit(solution)/shard_map/ppermute | solution.py:622
  12.7 94.0 %collective-permute-start.8 = (f32[1536]{0:T(1024)S(1)}, f32[1536]{0:T(1024)S(1)}, u32[]{:S(2)}, u32[]{:S(2)}) collective-permute-start(f32[1536]{0:T(1024)S(1)} %copy-done.80), channel_id=1, source_target_pairs={{0,1},{1,0},{2,3},{3,2},{4,5},{5,4},{6,7},{7,6},{8,9},{9,8},{10,11... | collective-permute-start | bytes 18440 | tf_op jit(solution)/shard_map/ppermute | solution.py:622
  20.0 33.4 %collective-permute-start.7 = (bf16[384,768]{1,0:T(8,128)(2,1)}, bf16[384,768]{1,0:T(8,128)(2,1)}, u32[]{:S(2)}, u32[]{:S(2)}) collective-permute-start(bf16[384,768]{1,0:T(8,128)(2,1)} %collective-permute-done.6), channel_id=1, source_target_pairs={{0,4},{2,6},{4,0},{6,2},{8,12},{10,14},{12,8},{14,10},{16,20},{18,... | collective-permute-start | bytes 1769480 | tf_op jit(solution)/shard_map/ppermute | solution.py:619
  48.8 31.6 %collective-permute-start.5 = (bf16[768,384]{1,0:T(8,128)(2,1)}, bf16[768,384]{1,0:T(8,128)(2,1)}, u32[]{:S(2)}, u32[]{:S(2)}) collective-permute-start(bf16[768,384]{1,0:T(8,128)(2,1)} %collective-permute-done.4), channel_id=1, source_target_pairs={{0,4},{2,6},{4,0},{6,2},{8,12},{10,14},{12,8},{14,10},{16,20},{18,... | collective-permute-start | bytes 1769480 | tf_op jit(solution)/shard_map/ppermute | solution.py:619
  50.5 29.9 %collective-permute-start.1 = (bf16[6,128,512]{2,1,0:T(8,128)(2,1)}, bf16[6,128,512]{2,1,0:T(8,128)(2,1)}, u32[]{:S(2)}, u32[]{:S(2)}) collective-permute-start(bf16[6,128,512]{2,1,0:T(8,128)(2,1)} %collective-permute-done.rest_0_.refs_5_), channel_id=1, source_target_pairs={{0,4},{2,6},{4,0},{6,2},{8,12},{10,14},{12,8},{14,10},{16,20},{18,... | collective-permute-start | bytes 2359304 | tf_op jit(solution)/shard_map/ppermute | solution.py:619
  53.4 53.4 %collective-permute-start.2 = (bf16[6,128,512]{2,1,0:T(8,128)(2,1)}, bf16[6,128,512]{2,1,0:T(8,128)(2,1)}, u32[]{:S(2)}, u32[]{:S(2)}) collective-permute-start(bf16[6,128,512]{2,1,0:T(8,128)(2,1)} %collective-permute-done.rest_0_.refs_5_), channel_id=1, source_target_pairs={{0,2},{2,0},{4,6},{6,4},{8,10},{10,8},{12,14},{14,12},{16,18},{18,... | collective-permute-start | bytes 2359304 | tf_op jit(solution)/shard_map/ppermute | solution.py:619
  55.9 104.5 %collective-permute-start.10 = (bf16[768,768]{1,0:T(8,128)(2,1)}, bf16[768,768]{1,0:T(8,128)(2,1)}, u32[]{:S(2)}, u32[]{:S(2)}) collective-permute-start(bf16[768,768]{1,0:T(8,128)(2,1)} %pad_maximum_fusion.2.refs_1_), channel_id=1, source_target_pairs={{0,2},{2,0},{4,6},{6,4},{8,10},{10,8},{12,14},{14,12},{16,18},{18,... | collective-permute-start | bytes 3538952 | tf_op jit(solution)/shard_map/ppermute | solution.py:619
  80.4 26.5 %collective-permute-start.3 = (bf16[6,128,512]{2,1,0:T(8,128)(2,1)}, bf16[6,128,512]{2,1,0:T(8,128)(2,1)}, u32[]{:S(2)}, u32[]{:S(2)}) collective-permute-start(bf16[6,128,512]{2,1,0:T(8,128)(2,1)} %collective-permute-done.1.rest_1_.refs_6_), channel_id=1, source_target_pairs={{0,2},{2,0},{4,6},{6,4},{8,10},{10,8},{12,14},{14,12},{16,18},{18,... | collective-permute-start | bytes 2359304 | tf_op jit(solution)/shard_map/ppermute | solution.py:619
  82.9 77.6 %collective-permute-start.9 = (bf16[768,768]{1,0:T(8,128)(2,1)}, bf16[768,768]{1,0:T(8,128)(2,1)}, u32[]{:S(2)}, u32[]{:S(2)}) collective-permute-start(bf16[768,768]{1,0:T(8,128)(2,1)} %pad_maximum_fusion.1.refs_0_), channel_id=1, source_target_pairs={{0,2},{2,0},{4,6},{6,4},{8,10},{10,8},{12,14},{14,12},{16,18},{18,... | collective-permute-start | bytes 3538952 | tf_op jit(solution)/shard_map/ppermute | solution.py:619
  262.1 95.9 %collective-permute-start.57 = (bf16[6,256,512]{2,1,0:T(8,128)(2,1)}, bf16[6,256,512]{2,1,0:T(8,128)(2,1)}, u32[]{:S(2)}, u32[]{:S(2)}) collective-permute-start(bf16[6,256,512]{2,1,0:T(8,128)(2,1)} %constant_dynamic-slice_fusion.4), channel_id=1, source_target_pairs={{0,2},{2,0},{4,6},{6,4},{8,10},{10,8},{12,14},{14,12},{16,18},{18,... | collective-permute-start | bytes 4718600 | tf_op jit(solution)/shard_map/ppermute | solution.py:619
  266.6 19.1 %collective-permute-start.27 = (bf16[384,384]{1,0:T(8,128)(2,1)S(1)}, bf16[384,384]{1,0:T(8,128)(2,1)S(1)}, u32[]{:S(2)}, u32[]{:S(2)}) collective-permute-start(bf16[384,384]{1,0:T(8,128)(2,1)S(1)} %convolution_convert_fusion.7), channel_id=1, source_target_pairs={{0,2},{2,0},{4,6},{6,4},{8,10},{10,8},{12,14},{14,12},{16,18},{18,... | collective-permute-start | bytes 884744 | tf_op jit(solution)/shard_map/ppermute | solution.py:619
  267.5 21.3 %collective-permute-start.26 = (bf16[384,384]{1,0:T(8,128)(2,1)S(1)}, bf16[384,384]{1,0:T(8,128)(2,1)S(1)}, u32[]{:S(2)}, u32[]{:S(2)}) collective-permute-start(bf16[384,384]{1,0:T(8,128)(2,1)S(1)} %convolution_convert_fusion.8), channel_id=1, source_target_pairs={{0,2},{2,0},{4,6},{6,4},{8,10},{10,8},{12,14},{14,12},{16,18},{18,... | collective-permute-start | bytes 884744 | tf_op jit(solution)/shard_map/ppermute | solution.py:619
  268.0 20.7 %collective-permute-start.21 = (f32[72,128]{1,0:T(8,128)S(1)}, f32[72,128]{1,0:T(8,128)S(1)}, u32[]{:S(2)}, u32[]{:S(2)}) collective-permute-start(f32[72,128]{1,0:T(8,128)S(1)} %bitcast.44), channel_id=1, source_target_pairs={{0,1},{1,0},{2,3},{3,2},{4,5},{5,4},{6,7},{7,6},{8,9},{9,8},{10,11... | collective-permute-start | bytes 110600 | tf_op jit(solution)/shard_map/ppermute | solution.py:622
  320.9 21.4 %collective-permute-start.13 = (bf16[384,1152]{1,0:T(8,128)(2,1)S(1)}, bf16[384,1152]{1,0:T(8,128)(2,1)S(1)}, u32[]{:S(2)}, u32[]{:S(2)}) collective-permute-start(bf16[384,1152]{1,0:T(8,128)(2,1)S(1)} %fusion.2), channel_id=1, source_target_pairs={{0,1},{1,0},{2,3},{3,2},{4,5},{5,4},{6,7},{7,6},{8,9},{9,8},{10,11... | collective-permute-start | bytes 2654216 | tf_op jit(solution)/shard_map/ppermute | solution.py:622
  327.0 102.6 %collective-permute-start.56 = (bf16[6,256,512]{2,1,0:T(8,128)(2,1)S(1)}, bf16[6,256,512]{2,1,0:T(8,128)(2,1)S(1)}, u32[]{:S(2)}, u32[]{:S(2)}) collective-permute-start(bf16[6,256,512]{2,1,0:T(8,128)(2,1)S(1)} %copy-done.79), channel_id=1, source_target_pairs={{0,2},{2,0},{4,6},{6,4},{8,10},{10,8},{12,14},{14,12},{16,18},{18,... | collective-permute-start | bytes 4718600 | tf_op jit(solution)/shard_map/ppermute | solution.py:619
  329.9 36.8 %collective-permute-start.46 = (bf16[768,768]{1,0:T(8,128)(2,1)S(1)}, bf16[768,768]{1,0:T(8,128)(2,1)S(1)}, u32[]{:S(2)}, u32[]{:S(2)}) collective-permute-start(bf16[768,768]{1,0:T(8,128)(2,1)S(1)} %copy-done.88), channel_id=1, source_target_pairs={{0,2},{2,0},{4,6},{6,4},{8,10},{10,8},{12,14},{14,12},{16,18},{18,... | collective-permute-start | bytes 3538952 | tf_op jit(solution)/shard_map/ppermute | solution.py:619
  347.7 54.9 %collective-permute-start.36 = (bf16[768,768]{1,0:T(8,128)(2,1)S(1)}, bf16[768,768]{1,0:T(8,128)(2,1)S(1)}, u32[]{:S(2)}, u32[]{:S(2)}) collective-permute-start(bf16[768,768]{1,0:T(8,128)(2,1)S(1)} %copy-done.89), channel_id=1, source_target_pairs={{0,2},{2,0},{4,6},{6,4},{8,10},{10,8},{12,14},{14,12},{16,18},{18,... | collective-permute-start | bytes 3538952 | tf_op jit(solution)/shard_map/ppermute | solution.py:619
  357.5 28.9 %collective-permute-start.48 = (bf16[768,768]{1,0:T(8,128)(2,1)S(1)}, bf16[768,768]{1,0:T(8,128)(2,1)S(1)}, u32[]{:S(2)}, u32[]{:S(2)}) collective-permute-start(bf16[768,768]{1,0:T(8,128)(2,1)S(1)} %add_convert_fusion.5), channel_id=1, source_target_pairs={{0,1},{1,0},{2,3},{3,2},{4,5},{5,4},{6,7},{7,6},{8,9},{9,8},{10,11... | collective-permute-start | bytes 3538952 | tf_op jit(solution)/shard_map/ppermute | solution.py:622
  364.9 46.7 %collective-permute-start.38 = (bf16[768,768]{1,0:T(8,128)(2,1)S(1)}, bf16[768,768]{1,0:T(8,128)(2,1)S(1)}, u32[]{:S(2)}, u32[]{:S(2)}) collective-permute-start(bf16[768,768]{1,0:T(8,128)(2,1)S(1)} %add_convert_fusion.7), channel_id=1, source_target_pairs={{0,1},{1,0},{2,3},{3,2},{4,5},{5,4},{6,7},{7,6},{8,9},{9,8},{10,11... | collective-permute-start | bytes 3538952 | tf_op jit(solution)/shard_map/ppermute | solution.py:622
  366.6 77.4 %collective-permute-start.58 = (bf16[6,256,512]{2,1,0:T(8,128)(2,1)S(1)}, bf16[6,256,512]{2,1,0:T(8,128)(2,1)S(1)}, u32[]{:S(2)}, u32[]{:S(2)}) collective-permute-start(bf16[6,256,512]{2,1,0:T(8,128)(2,1)S(1)} %add_convert_fusion.1), channel_id=1, source_target_pairs={{0,1},{1,0},{2,3},{3,2},{4,5},{5,4},{6,7},{7,6},{8,9},{9,8},{10,11... | collective-permute-start | bytes 4718600 | tf_op jit(solution)/shard_map/ppermute | solution.py:622
  413.8 35.9 %collective-permute-start.19 = (bf16[192,1152]{1,0:T(8,128)(2,1)S(1)}, bf16[192,1152]{1,0:T(8,128)(2,1)S(1)}, u32[]{:S(2)}, u32[]{:S(2)}) collective-permute-start(bf16[192,1152]{1,0:T(8,128)(2,1)S(1)} %pad_maximum_fusion.9), channel_id=1, source_target_pairs={{0,4},{2,6},{4,0},{6,2},{8,12},{10,14},{12,8},{14,10},{16,20},{18,... | collective-permute-start | bytes 1327112 | tf_op jit(solution)/shard_map/ppermute | solution.py:619
  414.6 31.8 %collective-permute-start.50 = (bf16[192,768]{1,0:T(8,128)(2,1)S(1)}, bf16[192,768]{1,0:T(8,128)(2,1)S(1)}, u32[]{:S(2)}, u32[]{:S(2)}) collective-permute-start(bf16[192,768]{1,0:T(8,128)(2,1)S(1)} %constant_dynamic-slice_fusion.7), channel_id=1, source_target_pairs={{0,8},{2,10},{4,12},{6,14},{8,0},{10,2},{12,4},{14,6},{16,24},{18,... | collective-permute-start | bytes 884744 | tf_op jit(solution)/shard_map/ppermute | solution.py:619
  428.6 19.0 %collective-permute-start.40 = (bf16[192,768]{1,0:T(8,128)(2,1)S(1)}, bf16[192,768]{1,0:T(8,128)(2,1)S(1)}, u32[]{:S(2)}, u32[]{:S(2)}) collective-permute-start(bf16[192,768]{1,0:T(8,128)(2,1)S(1)} %constant_dynamic-slice_fusion.10), channel_id=1, source_target_pairs={{0,8},{2,10},{4,12},{6,14},{8,0},{10,2},{12,4},{14,6},{16,24},{18,... | collective-permute-start | bytes 884744 | tf_op jit(solution)/shard_map/ppermute | solution.py:619
  444.8 29.2 %collective-permute-start.59 = (bf16[6,128,512]{2,1,0:T(8,128)(2,1)S(1)}, bf16[6,128,512]{2,1,0:T(8,128)(2,1)S(1)}, u32[]{:S(2)}, u32[]{:S(2)}) collective-permute-start(bf16[6,128,512]{2,1,0:T(8,128)(2,1)S(1)} %constant_dynamic-slice_fusion.3), channel_id=1, source_target_pairs={{0,4},{2,6},{4,0},{6,2},{8,12},{10,14},{12,8},{14,10},{16,20},{18,... | collective-permute-start | bytes 2359304 | tf_op jit(solution)/shard_map/ppermute | solution.py:619
  447.8 18.7 %collective-permute-start.41 = (bf16[96,768]{1,0:T(8,128)(2,1)S(1)}, bf16[96,768]{1,0:T(8,128)(2,1)S(1)}, u32[]{:S(2)}, u32[]{:S(2)}) collective-permute-start(bf16[96,768]{1,0:T(8,128)(2,1)S(1)} %constant_dynamic-slice_fusion.9), channel_id=1, source_target_pairs={{0,16},{2,18},{4,20},{6,22},{8,24},{10,26},{12,28},{14,30},{16,0},... | collective-permute-start | bytes 442376 | tf_op jit(solution)/shard_map/ppermute | solution.py:619
  449.9 52.0 %collective-permute-start.20 = (bf16[384,1152]{1,0:T(8,128)(2,1)S(1)}, bf16[384,1152]{1,0:T(8,128)(2,1)S(1)}, u32[]{:S(2)}, u32[]{:S(2)}) collective-permute-start(bf16[384,1152]{1,0:T(8,128)(2,1)S(1)} %pad_maximum_fusion.5), channel_id=1, source_target_pairs={{0,2},{2,0},{4,6},{6,4},{8,10},{10,8},{12,14},{14,12},{16,18},{18,... | collective-permute-start | bytes 2654216 | tf_op jit(solution)/shard_map/ppermute | solution.py:619
  474.4 22.5 %collective-permute-start.43 = (bf16[192,768]{1,0:T(8,128)(2,1)S(1)}, bf16[192,768]{1,0:T(8,128)(2,1)S(1)}, u32[]{:S(2)}, u32[]{:S(2)}) collective-permute-start(bf16[192,768]{1,0:T(8,128)(2,1)S(1)} %pad_maximum_fusion.12), channel_id=1, source_target_pairs={{0,8},{2,10},{4,12},{6,14},{8,0},{10,2},{12,4},{14,6},{16,24},{18,... | collective-permute-start | bytes 884744 | tf_op jit(solution)/shard_map/ppermute | solution.py:619
  481.5 27.2 %collective-permute-start.54 = (bf16[384,768]{1,0:T(8,128)(2,1)S(1)}, bf16[384,768]{1,0:T(8,128)(2,1)S(1)}, u32[]{:S(2)}, u32[]{:S(2)}) collective-permute-start(bf16[384,768]{1,0:T(8,128)(2,1)S(1)} %pad_maximum_fusion.8), channel_id=1, source_target_pairs={{0,4},{2,6},{4,0},{6,2},{8,12},{10,14},{12,8},{14,10},{16,20},{18,... | collective-permute-start | bytes 1769480 | tf_op jit(solution)/shard_map/ppermute | solution.py:619
  497.1 22.3 %collective-permute-start.44 = (bf16[384,768]{1,0:T(8,128)(2,1)S(1)}, bf16[384,768]{1,0:T(8,128)(2,1)S(1)}, u32[]{:S(2)}, u32[]{:S(2)}) collective-permute-start(bf16[384,768]{1,0:T(8,128)(2,1)S(1)} %pad_maximum_fusion.7), channel_id=1, source_target_pairs={{0,4},{2,6},{4,0},{6,2},{8,12},{10,14},{12,8},{14,10},{16,20},{18,... | collective-permute-start | bytes 1769480 | tf_op jit(solution)/shard_map/ppermute | solution.py:619
  509.0 28.7 %collective-permute-start.55 = (bf16[768,768]{1,0:T(8,128)(2,1)S(1)}, bf16[768,768]{1,0:T(8,128)(2,1)S(1)}, u32[]{:S(2)}, u32[]{:S(2)}) collective-permute-start(bf16[768,768]{1,0:T(8,128)(2,1)S(1)} %pad_maximum_fusion.4), channel_id=1, source_target_pairs={{0,2},{2,0},{4,6},{6,4},{8,10},{10,8},{12,14},{14,12},{16,18},{18,... | collective-permute-start | bytes 3538952 | tf_op jit(solution)/shard_map/ppermute | solution.py:619
  519.7 18.5 %collective-permute-start.45 = (bf16[768,768]{1,0:T(8,128)(2,1)S(1)}, bf16[768,768]{1,0:T(8,128)(2,1)S(1)}, u32[]{:S(2)}, u32[]{:S(2)}) collective-permute-start(bf16[768,768]{1,0:T(8,128)(2,1)S(1)} %pad_maximum_fusion.3), channel_id=1, source_target_pairs={{0,2},{2,0},{4,6},{6,4},{8,10},{10,8},{12,14},{14,12},{16,18},{18,... | collective-permute-start | bytes 3538952 | tf_op jit(solution)/shard_map/ppermute | solution.py:619
  (127 other events, 1187.2 us)
